TPU v7x, 512 devices: a whole 4x8x8 slice. The times are simulated.
512 devices in a mesh: ep: 64 (over x, y, core), tp: 8 (over z).
Axes of the slice: x: 4, y: 8, z: 8, core: 2. Of those that a mesh axis runs over, the one named last changes fastest.
Arguments:
- tokens_in: bfloat16 [1024, 3072], P('ep', 'tp'), may hold values from -6 to 6
- d_out: bfloat16 [1024, 3072], P('ep', 'tp'), may hold values from -2.390625 to 2.390625
- gates: float32 [1024, 2], P('ep'), may hold values from 0.2 to 1
- expert_ids: int32 [1024, 2], P('ep'), may hold values from 0 to 7, as said below
- slot_ids: int32 [1024, 2], P('ep'), may hold values from 0 to 5, as said below
- w_gate: bfloat16 [3072, 131072], P(None, ('ep', 'tp')), may hold values from -0.109375 to 0.109375
- w_up: bfloat16 [3072, 131072], P(None, ('ep', 'tp')), may hold values from -0.109375 to 0.109375
- w_down: bfloat16 [131072, 3072], P(('ep', 'tp')), may hold values from -0.046875 to 0.046875
Outputs:
- d_tokens: bfloat16 [1024, 3072], P('ep', 'tp')
- d_gates: float32 [1024, 2], P('ep')
Inputs may be any that keep to these rules, and one draw needn't show every extreme that they name: `expert_ids`: the two experts of a token differ. Within each block of tokens b * 16 to (b + 1) * 16 - 1, every expert is named by at most 6 rows, and one and the same expert is named by exactly 6 rows in every block. Rows of one block of 16 tokens that name the same expert have different slot_ids.
All inputs are finite; a program needn't handle non-finite values.
Results may differ from a plain program's by a relative error of at most 0.005.
Values may be sent and summed in bfloat16 or wider, within the bound.
A program may use at most 64 MiB of HBM per device.

v0:
```python
import jax
import jax.numpy as jnp
from jax import lax
from jax.sharding import PartitionSpec as P

EXPERTS = 8
CAP = 6


def slot_match(expert_ids, slot_ids, group_size, capacity, total_rows):
    position = jnp.arange(total_rows, dtype=jnp.int32)
    owner_expert = position // capacity // group_size
    slot_place = position % capacity
    same_expert = expert_ids[:, :, None] == owner_expert[None, None, :]
    same_slot = slot_ids[:, :, None] == slot_place[None, None, :]
    return (same_expert & same_slot).astype(jnp.float32)


def expert_terms(gate_pre, up_pre, back_grad):
    sigmoid_gate = jax.nn.sigmoid(gate_pre)
    silu_gate = gate_pre * sigmoid_gate
    scores = jnp.sum(silu_gate * up_pre * back_grad, axis=1)
    grad_gate = (
        back_grad * up_pre * sigmoid_gate * (1.0 + gate_pre * (1.0 - sigmoid_gate))
    ).astype(jnp.bfloat16)
    grad_up = (back_grad * silu_gate).astype(jnp.bfloat16)
    return (scores, grad_gate, grad_up)


def local(tokens_in, d_out, gates, expert_ids, slot_ids, w_gate, w_up, w_down):
    group_size = lax.axis_size("ep") // EXPERTS
    capacity = CAP
    total_rows = lax.axis_size("ep") * capacity
    match_values = slot_match(expert_ids, slot_ids, group_size, capacity, total_rows)
    dispatch_map = jnp.sum(match_values, axis=1).astype(jnp.bfloat16)
    combine_weights = jnp.sum(match_values * gates[:, :, None], axis=1)

    def spread(local_rows):
        placed = jnp.einsum(
            "tr,tf->rf", dispatch_map, local_rows, preferred_element_type=jnp.float32
        )
        return placed.astype(jnp.bfloat16)

    full_in, full_back = (
        lax.all_gather(tokens_in, "tp", axis=1, tiled=True),
        lax.all_gather(d_out, "tp", axis=1, tiled=True),
    )
    rows_in, rows_back = (
        lax.all_to_all(spread(full_in), "ep", split_axis=0, concat_axis=0, tiled=True),
        lax.all_to_all(spread(full_back), "ep", split_axis=0, concat_axis=0, tiled=True),
    )
    gate_pre = jnp.dot(rows_in, w_gate, preferred_element_type=jnp.float32)
    up_pre = jnp.dot(rows_in, w_up, preferred_element_type=jnp.float32)
    back_grad = lax.dot_general(
        rows_back, w_down, (((1,), (1,)), ((), ())), preferred_element_type=jnp.float32
    )
    scores, grad_gate, grad_up = expert_terms(gate_pre, up_pre, back_grad)
    partial_value = lax.dot_general(
        grad_gate, w_gate, (((1,), (1,)), ((), ())), preferred_element_type=jnp.float32
    )
    partial_value = partial_value + lax.dot_general(
        grad_up, w_up, (((1,), (1,)), ((), ())), preferred_element_type=jnp.float32
    )
    back_partial, back_scores = (
        lax.all_to_all(partial_value, "ep", split_axis=0, concat_axis=0, tiled=True),
        lax.all_to_all(scores, "ep", split_axis=0, concat_axis=0, tiled=True),
    )
    token_terms = jnp.dot(
        combine_weights,
        back_partial,
        precision=lax.Precision.HIGHEST,
        preferred_element_type=jnp.float32,
    )
    d_local = lax.psum_scatter(token_terms, "tp", scatter_dimension=1, tiled=True)
    gate_part = jnp.einsum("tkr,r->tk", match_values, back_scores, precision=lax.Precision.HIGHEST)
    d_gates = lax.psum(gate_part, "tp")
    return (d_local.astype(jnp.bfloat16), d_gates)


def solution(mesh):
    placed = (
        P("ep", "tp"),
        P("ep", "tp"),
        P("ep", None),
        P("ep", None),
        P("ep", None),
        P(None, ("ep", "tp")),
        P(None, ("ep", "tp")),
        P(("ep", "tp"), None),
    )
    return jax.shard_map(
        local, mesh=mesh, in_specs=placed, out_specs=(P("ep", "tp"), P("ep", None)), check_vma=False
    )
```

profile of v0, /device:TPU:6, one launch (start us, length us, event | category | flops | bytes accessed | tf_op | source)
XLA Modules:
  0.0 428.0 jit_solution(4357635520082627196)
XLA Ops:
  7.2 0.0 copy-start
  7.2 31.4 %all_gather.7 = bf16[16,3072]{1,0:T(8,128)(2,1)S(1)} all-gather(bf16[16,384]{1,0:T(8,128)(2,1)} %param.8), channel_id=1, replica_groups=mesh['ep'=64,'tp'=8] {'tp'}, dimensions={1}, use_global_device_ids=true | all-gather | bytes 110592 | tf_op jit(solution)/shard_map/all_gather | solution.py:45
  38.5 1.4 convert_reduce_fusion
  40.0 2.2 convolution_convert_fusion
  42.2 4.4 %all_to_all.35 = bf16[64,6,3072]{2,1,0:T(8,128)(2,1)} reshape(bf16[384,3072]{1,0:T(8,128)(2,1)} %convolution_convert_fusion) | data formatting | bytes 4718592 | tf_op jit(solution)/shard_map/all_to_all | solution.py:49
  46.5 0.0 copy-start.5
  46.5 11.1 %all-to-all-start.1 = ((bf16[64,6,3072]{2,1,0:T(8,128)(2,1)}), bf16[64,6,3072]{2,1,0:T(8,128)(2,1)}, u32[]{:S(2)}, u32[]{:S(2)}) async-start(bf16[64,6,3072]{2,1,0:T(8,128)(2,1)} %all_to_all.35), calls=%async_computation.1 | async-start | bytes 6291456 | tf_op jit(solution)/shard_map/all_to_all | solution.py:49
  57.7 0.0 copy-done.5
  57.7 24.7 %all_gather.6 = bf16[16,3072]{1,0:T(8,128)(2,1)S(1)} all-gather(bf16[16,384]{1,0:T(8,128)(2,1)S(1)} %copy-done.5), channel_id=1, replica_groups=mesh['ep'=64,'tp'=8] {'tp'}, dimensions={1}, use_global_device_ids=true | all-gather | bytes 110592 | tf_op jit(solution)/shard_map/all_gather | solution.py:46
  82.3 2.2 convolution_convert_fusion.1
  84.5 4.3 %all_to_all.32 = bf16[64,6,3072]{2,1,0:T(8,128)(2,1)} reshape(bf16[384,3072]{1,0:T(8,128)(2,1)} %convolution_convert_fusion.1) | data formatting | bytes 4718592 | tf_op jit(solution)/shard_map/all_to_all | solution.py:50
  88.8 40.1 %all-to-all-done.1 = bf16[64,6,3072]{2,1,0:T(8,128)(2,1)} async-done(((bf16[64,6,3072]{2,1,0:T(8,128)(2,1)}), bf16[64,6,3072]{2,1,0:T(8,128)(2,1)}, u32[]{:S(2)}, u32[]{:S(2)}) %all-to-all-start.1) | async-done | bytes 2359328 | tf_op jit(solution)/shard_map/all_to_all | solution.py:49
  129.0 8.4 %all-to-all-start = ((bf16[64,6,3072]{2,1,0:T(8,128)(2,1)}), bf16[64,6,3072]{2,1,0:T(8,128)(2,1)}, u32[]{:S(2)}, u32[]{:S(2)}) async-start(bf16[64,6,3072]{2,1,0:T(8,128)(2,1)} %all_to_all.32), calls=%async_computation | async-start | bytes 6291456 | tf_op jit(solution)/shard_map/all_to_all | solution.py:50
  137.4 0.0 reduce-scatter.2.cloned.1.call-start
  137.4 4.3 %all_to_all.37 = bf16[384,3072]{1,0:T(8,128)(2,1)} reshape(bf16[64,6,3072]{2,1,0:T(8,128)(2,1)} %all-to-all-done.1) | data formatting | bytes 4718592 | tf_op jit(solution)/shard_map/all_to_all | solution.py:49
  141.7 0.0 copy-done
  141.7 0.0 copy-start.1
  141.7 0.0 copy-start.2
  141.7 2.8 fusion.23
  144.6 0.0 copy-done.1
  144.6 0.0 copy-done.2
  144.6 1.8 fusion.22
  146.4 62.2 %all-to-all-done = bf16[64,6,3072]{2,1,0:T(8,128)(2,1)} async-done(((bf16[64,6,3072]{2,1,0:T(8,128)(2,1)}), bf16[64,6,3072]{2,1,0:T(8,128)(2,1)}, u32[]{:S(2)}, u32[]{:S(2)}) %all-to-all-start) | async-done | bytes 2359328 | tf_op jit(solution)/shard_map/all_to_all | solution.py:50
  208.7 4.4 %all_to_all.34 = bf16[384,3072]{1,0:T(8,128)(2,1)} reshape(bf16[64,6,3072]{2,1,0:T(8,128)(2,1)} %all-to-all-done) | data formatting | bytes 4718592 | tf_op jit(solution)/shard_map/all_to_all | solution.py:50
  213.0 0.0 copy-start.3
  213.0 3.2 multiply_reduce_fusion
  216.3 0.0 copy-done.3
  216.3 0.9 fusion.1
  217.2 3.1 convolution_add_fusion
  220.4 5.6 %all_to_all.38 = f32[64,6,3072]{2,1,0:T(8,128)} reshape(f32[384,3072]{1,0:T(8,128)} %convolution_add_fusion) | data formatting | bytes 9437184 | tf_op jit(solution)/shard_map/all_to_all | solution.py:65
  225.9 147.1 %all_to_all.48 = f32[64,6,3072]{2,1,0:T(8,128)} all-to-all(f32[64,6,3072]{2,1,0:T(8,128)} %all_to_all.38), channel_id=1, replica_groups=mesh['ep'=64,'tp'=8] {'ep'}, dimensions={0} | all-to-all | bytes 9437184 | tf_op jit(solution)/shard_map/all_to_all | solution.py:65
  373.1 0.0 copy-start.4
  373.1 5.5 %all_to_all.40 = f32[384,3072]{1,0:T(8,128)} reshape(f32[64,6,3072]{2,1,0:T(8,128)} %all_to_all.48) | data formatting | bytes 9437184 | tf_op jit(solution)/shard_map/all_to_all | solution.py:65
  378.6 0.0 copy-done.4
  378.6 0.0 copy-start.6
  378.6 5.4 %fusion.24 = f32[16,3072]{1,0:T(8,128)} fusion(f32[16,384]{1,0:T(8,128)S(1)} %copy-done.4, f32[384,3072]{1,0:T(8,128)} %all_to_all.40), kind=kOutput, calls=%fused_computation.42 | convolution fusion | flops 226492416 | bytes 4939776 | tf_op jit(solution)/shard_map/dot_general | solution.py:68
  384.0 0.0 reduce-scatter.2.cloned.1.call-update
  384.0 0.1 all_to_all.41
  384.2 15.5 %all_to_all.49 = f32[64,6,1]{1,2,0:T(1,128)S(1)} all-to-all(f32[64,6,1]{1,2,0:T(1,128)S(1)} %bitcast.20), channel_id=1, replica_groups=mesh['ep'=64,'tp'=8] {'ep'}, dimensions={0} | all-to-all | bytes 3072 | tf_op jit(solution)/shard_map/all_to_all | solution.py:66
  399.6 0.5 broadcast.92
  400.2 0.7 reduce.3
  400.9 0.1 reshape.49
  401.0 0.0 copy-done.6
  401.0 0.0 copy-done.7
  401.0 0.2 fusion.4
  401.3 17.4 %psum.7 = f32[16,2]{0,1:T(2,128)} all-reduce(f32[16,2]{0,1:T(2,128)S(1)} %bitcast.21), channel_id=1, replica_groups=mesh['ep'=64,'tp'=8] {'tp'}, use_global_device_ids=true, to_apply=%region_4.5 | all-reduce | flops 32 | bytes 256 | tf_op jit(solution)/shard_map/psum | solution.py:76
  418.7 1.1 reduce-scatter.2.cloned.1.call-done
  419.8 1.3 convert_element_type.27
  (2 shorter events, 0.0 us)
Async XLA Ops:
  7.2 134.6 %copy-start = (bf16[3072,256]{1,0:T(8,128)(2,1)S(1)}, bf16[3072,256]{1,0:T(8,128)(2,1)}, u32[]{:S(2)}) copy-start(bf16[3072,256]{1,0:T(8,128)(2,1)} %param.13) | copy-start | bytes 4718596
  46.5 11.1 %copy-start.5 = (bf16[16,384]{1,0:T(8,128)(2,1)S(1)}, bf16[16,384]{1,0:T(8,128)(2,1)}, u32[]{:S(2)}) copy-start(bf16[16,384]{1,0:T(8,128)(2,1)} %param.9) | copy-start | bytes 36868
  46.5 82.4 %all-to-all-start.1 = ((bf16[64,6,3072]{2,1,0:T(8,128)(2,1)}), bf16[64,6,3072]{2,1,0:T(8,128)(2,1)}, u32[]{:S(2)}, u32[]{:S(2)}) async-start(bf16[64,6,3072]{2,1,0:T(8,128)(2,1)} %all_to_all.35), calls=%async_computation.1 | async-start | bytes 6291456 | tf_op jit(solution)/shard_map/all_to_all | solution.py:49
  129.0 79.7 %all-to-all-start = ((bf16[64,6,3072]{2,1,0:T(8,128)(2,1)}), bf16[64,6,3072]{2,1,0:T(8,128)(2,1)}, u32[]{:S(2)}, u32[]{:S(2)}) async-start(bf16[64,6,3072]{2,1,0:T(8,128)(2,1)} %all_to_all.32), calls=%async_computation | async-start | bytes 6291456 | tf_op jit(solution)/shard_map/all_to_all | solution.py:50
  137.4 282.5 %reduce-scatter.2.cloned.1.call-start = ((), (), s32[]{:S(2)}) async-start(), calls=%async_computation.5 | async-start | bytes 221184 | tf_op jit(solution)/shard_map/reduce_scatter | solution.py:74
  141.7 2.9 copy-start.1
  141.7 2.9 copy-start.2
  213.0 3.2 copy-start.3
  373.1 5.5 %copy-start.4 = (f32[16,384]{1,0:T(8,128)S(1)}, f32[16,384]{1,0:T(8,128)}, u32[]{:S(2)}) copy-start(f32[16,384]{1,0:T(8,128)} %get-tuple-element.3) | copy-start | bytes 73732
  378.6 22.4 %copy-start.6 = (s32[16,2]{0,1:T(2,128)S(1)}, s32[16,2]{0,1:T(2,128)}, u32[]{:S(2)}) copy-start(s32[16,2]{0,1:T(2,128)} %param.12) | copy-start | bytes 388
  378.6 22.4 %copy-start.7 = (s32[16,2]{0,1:T(2,128)S(1)}, s32[16,2]{0,1:T(2,128)}, u32[]{:S(2)}) copy-start(s32[16,2]{0,1:T(2,128)} %param.11) | copy-start | bytes 388
Sparse Core Ops, SparseCore 0:
  384.1 35.6 reduce-scatter.1
where the time goes:
time: 429 us; the launch traced here: 428 us
  blocking collectives  236 us (55%)
  waiting for transfers between devices  103 us (24%)
  local copies, waits for them, and re-layouts  29.3 us (7%)
  matrix products  22 us (5%)
  starting transfers between devices  19.5 us (5%)
  between operations  14.2 us (3%)
    all_to_all x1, blocking collectives, local(): lax.all_to_all(partial_value, 'ep', split_axis=0, concat_axis=0, tiled=True)  147 us
    all_to_all x1, waiting for transfers between devices, local(): lax.all_to_all(spread(full_back), 'ep', split_axis=0, concat_axis=0, tile...  62.2 us
    all_to_all x1, waiting for transfers between devices, local(): lax.all_to_all(spread(full_in), 'ep', split_axis=0, concat_axis=0, tiled=...  40.1 us
    all_gather x1, blocking collectives, local(): lax.all_gather(tokens_in, 'tp', axis=1, tiled=True)  31.4 us
    all_gather x1, blocking collectives, local(): lax.all_gather(d_out, 'tp', axis=1, tiled=True)  24.7 us
    psum x1, blocking collectives, local(): d_gates = lax.psum(gate_part, 'tp')  17.4 us
    all_to_all x1, blocking collectives, local(): lax.all_to_all(scores, 'ep', split_axis=0, concat_axis=0, tiled=True)  15.5 us
    all_to_all x2, local copies, waits for them, and re-layouts, local(): lax.all_to_all(partial_value, 'ep', split_axis=0, concat_axis=0, tiled=True)  11.1 us
  transfers between devices with their start and end apart: 3, of which 3 were waited for; matrix products, arithmetic and copies ran while one was open for 2% of the time, Pallas kernels for 0%

commit v1 on v0

v1 whole, which is shorter than its diff:
```python
import jax
import jax.numpy as jnp
from jax import lax
from jax.experimental import pallas as pl
from jax.experimental.pallas import tpu as pltpu
from jax.sharding import PartitionSpec as P

MESH = pl.DeviceIdType.MESH
HIGH = lax.Precision.HIGHEST
EXPERTS = 8
CAP = 6
TOK = 16
NZ = 8
FEAT = 384
HID = 256
BLK = 48
HALF = 192
ROWS = 384
SUB = HALF // 2


def iota(shape, dim):
    return lax.broadcasted_iota(jnp.int32, shape, dim)


def div6(v):
    return (v * 43) >> 8


def kernel(
    tok, dout, gates, ids, slots, wg, wu, wd, d_tok, d_gate,
    wgu, wdn, send, drecv, G, acc_gu, acc_b, gcat, part, pair, rsend, rrecv, lsend, lrecv,
    total, ysend, yrecv, ret, rrecv2, scz, scy, scc, scs,
    w_sem, d_ss, d_rs, y_ss, y_rs, r_ss, r_rs, l_ss, l_rs, f_ss, f_rs,
    p_ss, p_rs, rr_ss, rr_rs, rl_ss, rl_rs, yy_ss, yy_rs, t_ss, t_rs, z_ss, z_rs, s_ss, s_rs, c_ss, c_rs,
):
    ep = lax.axis_index("ep")
    z = lax.axis_index("tp")
    own = lax.div(ep, 8)
    place = lax.rem(ep, 8)
    yl = lax.div(place, 2)
    c = lax.rem(place, 2)
    other = 1 - c

    def at_expert(e):
        return (e * 8 + place, z)

    def at_y(yy):
        return (own * 8 + yy * 2 + c, z)

    def at_z(zz):
        return (ep, zz)

    sibling = (own * 8 + yl * 2 + other, z)

    def copy(src, dst, ss, rs, dev):
        return pltpu.make_async_remote_copy(
            src_ref=src, dst_ref=dst, send_sem=ss, recv_sem=rs, device_id=dev, device_id_type=MESH
        )

    loads = [
        pltpu.make_async_copy(wg, wgu.at[:, pl.ds(0, HID)], w_sem.at[0]),
        pltpu.make_async_copy(wu, wgu.at[:, pl.ds(HID, HID)], w_sem.at[1]),
        pltpu.make_async_copy(wd, wdn, w_sem.at[2]),
    ]
    for ld in loads:
        ld.start()

    barrier = pltpu.get_barrier_semaphore()
    peers = [at_expert(lax.rem(own + i, 8)) for i in range(1, 8)]
    peers += [at_y(lax.rem(yl + i, 4)) for i in range(1, 4)]
    peers += [at_z(lax.rem(z + i, NZ)) for i in range(1, NZ)]
    peers += [sibling]
    for dev in peers:
        pl.semaphore_signal(barrier, inc=1, device_id=dev, device_id_type=MESH)

    r = iota((128, TOK), 0)
    pick = jnp.zeros((128, TOK), jnp.float32)
    for k in range(2):
        hit = (ids[k : k + 1, :] == (r >> 4)) & (slots[k : k + 1, :] == (r & 7))
        pick = pick + hit.astype(jnp.float32)
    is_back = (r & 8) == 8
    pick_in = jnp.where(is_back, 0.0, pick).astype(jnp.bfloat16)
    pick_back = jnp.where(is_back, pick, 0.0).astype(jnp.bfloat16)
    placed = jnp.dot(pick_in, tok[...], preferred_element_type=jnp.float32)
    placed = placed + jnp.dot(pick_back, dout[...], preferred_element_type=jnp.float32)
    send[...] = placed.astype(jnp.bfloat16).reshape(EXPERTS, 16, FEAT)

    pl.semaphore_wait(barrier, len(peers))

    waits = []
    disp = []
    for i in range(1, 8):
        e = lax.rem(own + i, 8)
        cp = copy(send.at[e], drecv.at[own], d_ss.at[i], d_rs.at[i], at_expert(e))
        cp.start()
        disp.append(cp)
    drecv[own] = send[own]
    for i in range(1, 8):
        j = lax.rem(own + 8 - i, 8)
        copy(send.at[j], drecv.at[j], d_ss.at[i], d_rs.at[i], at_expert(j)).wait_recv()
    waits += disp

    r = iota((2 * BLK, 128), 0)
    back = (r >= BLK).astype(jnp.int32)
    q = r - back * BLK
    j6 = div6(q)
    sel = (iota((2 * BLK, 128), 1) == j6 * 16 + back * 8 + (q - 6 * j6)).astype(jnp.bfloat16)
    dense = jnp.dot(sel, drecv[...].reshape(128, FEAT), preferred_element_type=jnp.float32)
    dense = dense.astype(jnp.bfloat16)
    G[z, 0, c, yl] = dense[:BLK]
    G[z, 1, c, yl] = dense[BLK:]

    for i in range(1, 4):
        yy = lax.rem(yl + i, 4)
        blk = G.at[z, :, c, yl]
        cp = copy(blk, blk, y_ss.at[i], y_rs.at[i], at_y(yy))
        cp.start()
        waits.append(cp)
    for i in range(1, 4):
        yy = lax.rem(yl + 4 - i, 4)
        blk = G.at[z, :, c, yy]
        copy(blk, blk, y_ss.at[i], y_rs.at[i], at_y(yy)).wait_recv()

    acc_gu[...] = jnp.zeros_like(acc_gu)
    acc_b[...] = jnp.zeros_like(acc_b)

    def right(k, a):
        blk = G.at[lax.rem(z + NZ - k, NZ), a, c]
        return copy(blk, blk, r_ss.at[k, a], r_rs.at[k, a], at_z(lax.rem(z + 1, NZ)))

    def right_got(k, a):
        blk = G.at[lax.rem(z + NZ - 1 - k, NZ), a, c]
        return copy(blk, blk, r_ss.at[k, a], r_rs.at[k, a], at_z(lax.rem(z + 1, NZ)))

    def left(k, a):
        blk = G.at[lax.rem(z + k, NZ), a, c]
        return copy(blk, blk, l_ss.at[k, a], l_rs.at[k, a], at_z(lax.rem(z + NZ - 1, NZ)))

    def left_got(k, a):
        blk = G.at[lax.rem(z + k + 1, NZ), a, c]
        return copy(blk, blk, l_ss.at[k, a], l_rs.at[k, a], at_z(lax.rem(z + NZ - 1, NZ)))

    def forward(slot, a, n):
        blk = G.at[slot, a, c]
        return copy(blk, blk, f_ss.at[n, a], f_rs.at[n, a], sibling)

    def forwarded(slot, a, n):
        blk = G.at[slot, a, other]
        return copy(blk, blk, f_ss.at[n, a], f_rs.at[n, a], sibling)

    def slot_of(n):
        if n == 0:
            return z
        if n <= 3:
            return lax.rem(z + NZ - n, NZ)
        if n <= 6:
            return lax.rem(z + n - 3, NZ)
        return lax.rem(z + 4, NZ)

    def products(slot):
        base = pl.multiple_of(slot * FEAT, FEAT)
        rows_in = G[slot, 0].reshape(ROWS, FEAT)
        rows_back = G[slot, 1].reshape(ROWS, FEAT)
        acc_gu[...] += jnp.dot(
            rows_in, wgu[pl.ds(base, FEAT), :], preferred_element_type=jnp.float32
        )
        acc_b[...] += lax.dot_general(
            rows_back, wdn[:, pl.ds(base, FEAT)], (((1,), (1,)), ((), ())),
            preferred_element_type=jnp.float32,
        )

    def start(cp):
        cp.start()
        waits.append(cp)

    for a in range(2):
        start(right(0, a))
        start(left(0, a))
        start(forward(z, a, 0))
    for ld in loads:
        ld.wait()
    for k in range(4):
        ready = [0] if k == 0 else [k, k + 3]
        if k < 3:
            for a in range(2):
                right_got(k, a).wait_recv()
                if k < 2 or a == 0:
                    start(right(k + 1, a))
                start(forward(slot_of(k + 1), a, k + 1))
                left_got(k, a).wait_recv()
                if k < 2 or a == 1:
                    start(left(k + 1, a))
                start(forward(slot_of(k + 4), a, k + 4))
        else:
            right_got(3, 0).wait_recv()
            start(forward(slot_of(7), 0, 7))
            left_got(3, 1).wait_recv()
            start(forward(slot_of(7), 1, 7))
            ready = ready + [7]
        for n in ready:
            for a in range(2):
                forwarded(slot_of(n), a, n).wait_recv()
            products(slot_of(n))

    gate = acc_gu[:, :HID]
    up = acc_gu[:, HID:]
    bg = acc_b[...]
    sg = jax.nn.sigmoid(gate)
    silu = gate * sg
    gcat[:, :HID] = (bg * up * sg * (1.0 + gate * (1.0 - sg))).astype(jnp.bfloat16)
    gcat[:, HID:] = (bg * silu).astype(jnp.bfloat16)
    score = jnp.sum(silu * up * bg, axis=1, keepdims=True)

    q = iota((ROWS, 128), 0)
    for v in (4, 2, 1):
        q = jnp.where(q >= v * BLK, q - v * BLK, q)
    j6 = div6(q)
    spread = jnp.where(iota((ROWS, 128), 1) == j6 * 8 + (q - 6 * j6), score, 0.0)
    g = iota((8, ROWS), 0)
    n = iota((8, ROWS), 1)
    mine = ((n >= g * BLK) & (n < g * BLK + BLK)).astype(jnp.float32)
    scz[z] = jnp.dot(mine, spread, precision=HIGH, preferred_element_type=jnp.float32)
    for i in range(1, NZ):
        zz = lax.rem(z + i, NZ)
        start(copy(scz.at[z], scz.at[z], z_ss.at[i], z_rs.at[i], at_z(zz)))

    def slice_grad(slot):
        base = pl.multiple_of(slot * FEAT, FEAT)
        part[slot] = lax.dot_general(
            gcat[...], wgu[pl.ds(base, FEAT), :], (((1,), (1,)), ((), ())),
            preferred_element_type=jnp.float32,
        ).reshape(2, HALF, FEAT)

    def pair_send(slot, n):
        return copy(part.at[slot, other], pair.at[slot], p_ss.at[n], p_rs.at[n], sibling)

    order = [7, 3, 6, 2, 5, 1, 4, 0]
    for n in order:
        slice_grad(slot_of(n))
        start(pair_send(slot_of(n), n))

    def pair_sum(n, lo, size):
        slot = slot_of(n)
        return part[slot, c, lo : lo + size, :] + pair[slot, lo : lo + size, :]

    def pair_wait(n):
        pair_send(slot_of(n), n).wait_recv()

    def ring_r(k):
        rows = pl.ds(0, SUB) if k == 0 else pl.ds(0, HALF)
        return copy(
            rsend.at[k, rows], rrecv.at[k, rows], rr_ss.at[k], rr_rs.at[k],
            at_z(lax.rem(z + 1, NZ)),
        )

    def ring_l(k):
        rows = pl.ds(SUB, SUB) if k == 0 else pl.ds(0, HALF)
        return copy(
            lsend.at[k, rows], lrecv.at[k, rows], rl_ss.at[k], rl_rs.at[k],
            at_z(lax.rem(z + NZ - 1, NZ)),
        )

    pair_wait(7)
    rsend[0, :SUB] = pair_sum(7, 0, SUB).astype(jnp.bfloat16)
    start(ring_r(0))
    lsend[0, SUB:] = pair_sum(7, SUB, SUB).astype(jnp.bfloat16)
    start(ring_l(0))
    for k in range(1, 4):
        nr, nl = 7 - k, 4 - k
        pair_wait(nr)
        pair_wait(nl)
        if k == 1:
            rsend[1, SUB:] = pair_sum(nr, SUB, SUB).astype(jnp.bfloat16)
            lsend[1, :SUB] = pair_sum(nl, 0, SUB).astype(jnp.bfloat16)
            ring_r(0).wait_recv()
            rsend[1, :SUB] = (pair_sum(nr, 0, SUB) + rrecv[0, :SUB].astype(jnp.float32)).astype(
                jnp.bfloat16
            )
            start(ring_r(1))
            ring_l(0).wait_recv()
            lsend[1, SUB:] = (
                pair_sum(nl, SUB, SUB) + lrecv[0, SUB:].astype(jnp.float32)
            ).astype(jnp.bfloat16)
            start(ring_l(1))
        else:
            ring_r(k - 1).wait_recv()
            rsend[k] = (pair_sum(nr, 0, HALF) + rrecv[k - 1].astype(jnp.float32)).astype(
                jnp.bfloat16
            )
            start(ring_r(k))
            ring_l(k - 1).wait_recv()
            lsend[k] = (pair_sum(nl, 0, HALF) + lrecv[k - 1].astype(jnp.float32)).astype(
                jnp.bfloat16
            )
            start(ring_l(k))
        if k == 2:
            for i in range(1, NZ):
                zz = lax.rem(z + NZ - i, NZ)
                copy(scz.at[zz], scz.at[zz], z_ss.at[i], z_rs.at[i], at_z(zz)).wait_recv()
            scy[yl] = jnp.sum(scz[...], axis=0)
            for i in range(1, 4):
                yy = lax.rem(yl + i, 4)
                start(copy(scy.at[yl], scy.at[yl], s_ss.at[i], s_rs.at[i], at_y(yy)))
        if k == 3:
            for i in range(1, 4):
                yy = lax.rem(yl + 4 - i, 4)
                copy(scy.at[yy], scy.at[yy], s_ss.at[i], s_rs.at[i], at_y(yy)).wait_recv()
            scc[c] = jnp.sum(scy[...], axis=0)
            start(copy(scc.at[c], scc.at[c], c_ss, c_rs, sibling))
    pair_wait(0)
    copy(scc.at[other], scc.at[other], c_ss, c_rs, sibling).wait_recv()
    scs[...] = scc[0] + scc[1]
    ring_r(3).wait_recv()
    ring_l(3).wait_recv()
    summed = pair_sum(0, 0, HALF) + rrecv[3].astype(jnp.float32) + lrecv[3].astype(jnp.float32)
    total[...] = summed.reshape(4, BLK, FEAT)
    ysend[...] = summed.astype(jnp.bfloat16).reshape(4, BLK, FEAT)
    for i in range(1, 4):
        yy = lax.rem(yl + i, 4)
        start(copy(ysend.at[yy], yrecv.at[i], yy_ss.at[i], yy_rs.at[i], at_y(yy)))
    rows = total[yl]
    for i in range(1, 4):
        copy(ysend.at[0], yrecv.at[i], yy_ss.at[i], yy_rs.at[i], at_y(yl)).wait_recv()
        rows = rows + yrecv[i].astype(jnp.float32)

    r = iota((64, BLK), 0)
    pos = iota((64, BLK), 1)
    sel = (((r & 7) < CAP) & (pos == (r >> 3) * 6 + (r & 7))).astype(jnp.float32)
    ret[:, :, :FEAT] = jnp.dot(
        sel, rows, precision=HIGH, preferred_element_type=jnp.float32
    ).reshape(EXPERTS, 8, FEAT)
    ret[:, :, FEAT:] = jnp.broadcast_to(scs[...][None], (EXPERTS, 8, 128))
    for i in range(1, 8):
        e = lax.rem(own + i, 8)
        start(copy(ret.at[e], rrecv2.at[own], t_ss.at[i], t_rs.at[i], at_expert(e)))
    rrecv2[own] = ret[own]
    r = iota((64, TOK), 0)
    hits = []
    weight = jnp.zeros((64, TOK), jnp.float32)
    for k in range(2):
        hit = (ids[k : k + 1, :] == (r >> 3)) & (slots[k : k + 1, :] == (r & 7))
        hits.append(hit)
        weight = weight + jnp.where(hit, gates[k : k + 1, :], 0.0)
    for i in range(1, 8):
        j = lax.rem(own + 8 - i, 8)
        copy(ret.at[j], rrecv2.at[j], t_ss.at[i], t_rs.at[i], at_expert(j)).wait_recv()
    d_tok[...] = lax.dot_general(
        weight, rrecv2[:, :, :FEAT].reshape(64, FEAT), (((0,), (0,)), ((), ())),
        precision=HIGH, preferred_element_type=jnp.float32,
    ).astype(jnp.bfloat16)
    sc = rrecv2[:, :, FEAT:]
    row = c * 4 + yl
    sc = jnp.sum(jnp.where(iota((EXPERTS, 8, 128), 1) == row, sc, 0.0), axis=1, keepdims=True)
    sc = jnp.broadcast_to(sc, (EXPERTS, 8, 128)).reshape(64, 128)
    lane = own * 8 + (iota((64, 128), 0) & 7)
    sc = jnp.sum(jnp.where(iota((64, 128), 1) == lane, sc, 0.0), axis=1, keepdims=True)
    for k in range(2):
        d_gate[k : k + 1, :] = jnp.sum(jnp.where(hits[k], sc, 0.0), axis=0, keepdims=True)
    for cp in waits:
        cp.wait_send()


def local(tokens_in, d_out, gates, expert_ids, slot_ids, w_gate, w_up, w_down):
    vmem = pl.BlockSpec(memory_space=pltpu.VMEM)
    hbm = pl.BlockSpec(memory_space=pl.ANY)
    bf, f32, dma = jnp.bfloat16, jnp.float32, pltpu.SemaphoreType.DMA
    scratch = [
        pltpu.VMEM((NZ * FEAT, 2 * HID), bf),
        pltpu.VMEM((HID, NZ * FEAT), bf),
        pltpu.VMEM((EXPERTS, 16, FEAT), bf),
        pltpu.VMEM((EXPERTS, 16, FEAT), bf),
        pltpu.VMEM((NZ, 2, 2, 4, BLK, FEAT), bf),
        pltpu.VMEM((ROWS, 2 * HID), f32),
        pltpu.VMEM((ROWS, HID), f32),
        pltpu.VMEM((ROWS, 2 * HID), bf),
        pltpu.VMEM((NZ, 2, HALF, FEAT), f32),
        pltpu.VMEM((NZ, HALF, FEAT), f32),
        pltpu.VMEM((4, HALF, FEAT), bf),
        pltpu.VMEM((4, HALF, FEAT), bf),
        pltpu.VMEM((4, HALF, FEAT), bf),
        pltpu.VMEM((4, HALF, FEAT), bf),
        pltpu.VMEM((4, BLK, FEAT), f32),
        pltpu.VMEM((4, BLK, FEAT), bf),
        pltpu.VMEM((4, BLK, FEAT), bf),
        pltpu.VMEM((EXPERTS, 8, FEAT + 128), f32),
        pltpu.VMEM((EXPERTS, 8, FEAT + 128), f32),
        pltpu.VMEM((NZ, 8, 128), f32),
        pltpu.VMEM((4, 8, 128), f32),
        pltpu.VMEM((2, 8, 128), f32),
        pltpu.VMEM((8, 128), f32),
        dma((3,)),
        dma((8,)), dma((8,)),
        dma((4,)), dma((4,)),
        dma((4, 2)), dma((4, 2)),
        dma((4, 2)), dma((4, 2)),
        dma((8, 2)), dma((8, 2)),
        dma((8,)), dma((8,)),
        dma((4,)), dma((4,)),
        dma((4,)), dma((4,)),
        dma((4,)), dma((4,)),
        dma((8,)), dma((8,)),
        dma((8,)), dma((8,)),
        dma((4,)), dma((4,)),
        dma, dma,
    ]
    d_tok, d_gate = pl.pallas_call(
        kernel,
        out_shape=(
            jax.ShapeDtypeStruct((TOK, FEAT), bf),
            jax.ShapeDtypeStruct((2, TOK), f32),
        ),
        in_specs=[vmem] * 5 + [hbm] * 3,
        out_specs=(vmem, vmem),
        scratch_shapes=scratch,
        name="moe_dx",
        compiler_params=pltpu.CompilerParams(
            collective_id=0, has_side_effects=True, vmem_limit_bytes=48 * 2**20
        ),
        cost_estimate=pl.CostEstimate(
            flops=5 * 2 * ROWS * NZ * FEAT * HID, bytes_accessed=6 * NZ * FEAT * HID, transcendentals=ROWS * HID
        ),
    )(tokens_in, d_out, gates.T, expert_ids.T, slot_ids.T, w_gate, w_up, w_down)
    return d_tok, d_gate.T


def solution(mesh):
    placed = (
        P("ep", "tp"),
        P("ep", "tp"),
        P("ep", None),
        P("ep", None),
        P("ep", None),
        P(None, ("ep", "tp")),
        P(None, ("ep", "tp")),
        P(("ep", "tp"), None),
    )
    return jax.shard_map(
        local, mesh=mesh, in_specs=placed, out_specs=(P("ep", "tp"), P("ep", None)), check_vma=False
    )
```

time: 429 us -> 102 us (0.24)
  the two profiles are of different devices: /device:TPU:6 before, /device:TPU:16 now
where the time goes in v1:
time: 102 us
  Pallas kernels  92.2 us (90%)
  local copies, waits for them, and re-layouts  8.83 us (9%)
    pallas_call x1, Pallas kernels, local(): pl.pallas_call(kernel, out_shape=(jax.ShapeDtypeStruct((TOK, FEAT), bf),...  92.2 us
    unnamed x18, local copies, waits for them, and re-layouts  8.83 us

profile of v1, /device:TPU:16, one launch (start us, length us, event | category | flops | bytes accessed | tf_op | source)
XLA Modules:
  0.0 101.7 jit_solution(13321271383300059571)
XLA Ops:
  0.6 0.0 copy-start
  0.6 1.4 %copy-done = bf16[3072,256]{1,0:T(8,128)(2,1)S(1)} copy-done((bf16[3072,256]{1,0:T(8,128)(2,1)S(1)}, bf16[3072,256]{1,0:T(8,128)(2,1)}, u32[]{:S(2)}) %copy-start) | copy-done | bytes 1572888
  2.0 0.0 copy-start.1
  2.0 1.4 %copy-done.1 = bf16[3072,256]{1,0:T(8,128)(2,1)S(1)} copy-done((bf16[3072,256]{1,0:T(8,128)(2,1)S(1)}, bf16[3072,256]{1,0:T(8,128)(2,1)}, u32[]{:S(2)}) %copy-start.1) | copy-done | bytes 1572888
  3.5 0.0 copy-start.2
  3.5 1.4 %copy-done.2 = bf16[256,3072]{1,0:T(8,128)(2,1)S(1)} copy-done((bf16[256,3072]{1,0:T(8,128)(2,1)S(1)}, bf16[256,3072]{1,0:T(8,128)(2,1)}, u32[]{:S(2)}) %copy-start.2) | copy-done | bytes 1572888
  4.9 0.0 copy-start.3
  4.9 0.7 copy-done.3
  5.6 0.0 copy-start.4
  5.6 0.7 copy-done.4
  6.3 0.0 copy-start.5
  6.3 0.7 copy-done.5
  7.0 0.0 copy-start.6
  7.0 0.7 copy-done.6
  7.6 0.0 copy-start.7
  7.6 0.7 copy-done.7
  8.3 92.2 %moe_dx.1 = (bf16[16,384]{1,0:T(8,128)(2,1)S(1)}, f32[2,16]{1,0:T(2,128)S(1)}) custom-call(bf16[16,384]{1,0:T(8,128)(2,1)S(1)} %copy-done.3, bf16[16,384]{1,0:T(8,128)(2,1)S(1)} %copy-done.4, f32[2,16]{1,0:T(2,128)S(1)} %bitcast.5, s32[2,16]{1,0:T(2,128)S(1)} %bitcast.6, s32[2,16]{1,0:T(2,128)S(1)} %bitcast.7, bf16[3072,256]{1,0:T(8,128)(2,1)S(1)} %copy-done, ...), custom_call_target="tpu_custom_call" | custom-call | flops 3019898880 | bytes 4718592 | tf_op jit(solution)/shard_map/moe_dx/pallas_call | solution.py:407
  100.5 0.6 copy.12
  101.1 0.6 copy.13
Async XLA Ops:
  0.6 1.4 %copy-start = (bf16[3072,256]{1,0:T(8,128)(2,1)S(1)}, bf16[3072,256]{1,0:T(8,128)(2,1)}, u32[]{:S(2)}) copy-start(bf16[3072,256]{1,0:T(8,128)(2,1)} %wg.1) | copy-start | bytes 4718596
  2.0 1.4 %copy-start.1 = (bf16[3072,256]{1,0:T(8,128)(2,1)S(1)}, bf16[3072,256]{1,0:T(8,128)(2,1)}, u32[]{:S(2)}) copy-start(bf16[3072,256]{1,0:T(8,128)(2,1)} %wu.1) | copy-start | bytes 4718596
  3.5 1.4 %copy-start.2 = (bf16[256,3072]{1,0:T(8,128)(2,1)S(1)}, bf16[256,3072]{1,0:T(8,128)(2,1)}, u32[]{:S(2)}) copy-start(bf16[256,3072]{1,0:T(8,128)(2,1)} %wd.1) | copy-start | bytes 4718596
  4.9 0.7 copy-start.3
  5.6 0.7 copy-start.4
  6.3 0.7 copy-start.5
  7.0 0.7 copy-start.6
  7.6 0.7 copy-start.7

commit v2 on v1

v2 whole, which is shorter than its diff:
```python
import jax
import jax.numpy as jnp
from jax import lax
from jax.experimental import pallas as pl
from jax.experimental.pallas import tpu as pltpu
from jax.sharding import PartitionSpec as P

MESH = pl.DeviceIdType.MESH
HIGH = lax.Precision.HIGHEST
EXPERTS = 8
CAP = 6
TOK = 16
NZ = 8
FEAT = 384
HID = 256
BLK = 48
HALF = 192
SUB = HALF // 2


def iota(shape, dim):
    return lax.broadcasted_iota(jnp.int32, shape, dim)


def div6(v):
    return (v * 43) >> 8


def kernel(
    tok_h, dout_h, gates_h, ids_h, slots_h, wg, wu, wd, d_tok, d_gate,
    tok, dout, gates, ids, slots, wgu, wdn, send, drecv, G, acc_gu, acc_b, gcat, part,
    rsend, rrecv, lsend, lrecv, total, ysend, yrecv, ret, back, scz, scy, scs,
    i_sem, w_sem, p_ss, p_rs, d_ss, d_rs, y_ss, y_rs, r_ss, r_rs, l_ss, l_rs,
    rr_ss, rr_rs, rl_ss, rl_rs, yy_ss, yy_rs, t_ss, t_rs, z_ss, z_rs, s_ss, s_rs,
):
    ep = lax.axis_index("ep")
    z = lax.axis_index("tp")
    own = lax.div(ep, 8)
    place = lax.rem(ep, 8)
    yl = lax.div(place, 2)
    c = lax.rem(place, 2)

    def at_expert(e):
        mirrored = lax.rem(own + e, 2)
        return (e * 8 + (yl + mirrored * (3 - 2 * yl)) * 2 + c, z)

    def at_y(yy):
        return (own * 8 + yy * 2 + c, z)

    def at_z(zz):
        return (ep, zz)

    sibling = (own * 8 + yl * 2 + 1 - c, z)

    def copy(src, dst, ss, rs, dev):
        return pltpu.make_async_remote_copy(
            src_ref=src, dst_ref=dst, send_sem=ss, recv_sem=rs, device_id=dev, device_id_type=MESH
        )

    waits = []

    def start(cp):
        cp.start()
        waits.append(cp)

    def weights(core):
        at = pl.multiple_of(core * HID, HID)
        return (
            (wg, wgu.at[:, pl.ds(at, HID)]),
            (wu, wgu.at[:, pl.ds(pl.multiple_of(at + 2 * HID, HID), HID)]),
            (wd, wdn.at[pl.ds(at, HID), :]),
        )

    small = [
        pltpu.make_async_copy(src, dst, i_sem.at[i])
        for i, (src, dst) in enumerate(
            ((ids_h, ids), (slots_h, slots), (tok_h, tok), (dout_h, dout), (gates_h, gates))
        )
    ]
    loads = [
        pltpu.make_async_copy(src, dst, w_sem.at[i]) for i, (src, dst) in enumerate(weights(c))
    ]
    for ld in small + loads:
        ld.start()

    barrier = pltpu.get_barrier_semaphore()
    peers = [at_expert(lax.rem(own + i, 8)) for i in range(1, 8)]
    peers += [at_y(lax.rem(yl + i, 4)) for i in range(1, 4)]
    peers += [at_z(lax.rem(z + i, NZ)) for i in range(1, NZ)]
    peers += [sibling]
    for dev in peers:
        pl.semaphore_signal(barrier, inc=1, device_id=dev, device_id_type=MESH)

    for ld in small:
        ld.wait()
    r = iota((128, TOK), 0)
    pick = jnp.zeros((128, TOK), jnp.float32)
    for k in range(2):
        hit = (ids[k : k + 1, :] == (r >> 4)) & (slots[k : k + 1, :] == (r & 7))
        pick = pick + hit.astype(jnp.float32)
    is_back = (r & 8) == 8
    pick_in = jnp.where(is_back, 0.0, pick).astype(jnp.bfloat16)
    pick_back = jnp.where(is_back, pick, 0.0).astype(jnp.bfloat16)
    placed = jnp.dot(pick_in, tok[...], preferred_element_type=jnp.float32)
    placed = placed + jnp.dot(pick_back, dout[...], preferred_element_type=jnp.float32)
    send[...] = placed.astype(jnp.bfloat16).reshape(EXPERTS, 16, FEAT)

    pl.semaphore_wait(barrier, len(peers))

    for i in range(1, 8):
        e = lax.rem(own + i, 8)
        start(copy(send.at[e], drecv.at[own], d_ss.at[i], d_rs.at[i], at_expert(e)))
    for i, (src, dst) in enumerate(weights(c)):
        start(copy(src, dst, p_ss.at[i], p_rs.at[i], sibling))
    drecv[own] = send[own]
    r = iota((2 * BLK, 128), 0)
    second = (r >= BLK).astype(jnp.int32)
    q = r - second * BLK
    j6 = div6(q)
    sel = (iota((2 * BLK, 128), 1) == j6 * 16 + second * 8 + (q - 6 * j6)).astype(jnp.bfloat16)
    for i in range(1, 8):
        j = lax.rem(own + 8 - i, 8)
        copy(send.at[j], drecv.at[j], d_ss.at[i], d_rs.at[i], at_expert(j)).wait_recv()
    dense = jnp.dot(sel, drecv[...].reshape(128, FEAT), preferred_element_type=jnp.float32)
    dense = dense.astype(jnp.bfloat16)
    G[z, 0, yl] = dense[:BLK]
    G[z, 1, yl] = dense[BLK:]

    for i in range(1, 4):
        yy = lax.rem(yl + i, 4)
        blk = G.at[z, :, yl]
        start(copy(blk, blk, y_ss.at[i], y_rs.at[i], at_y(yy)))
    acc_gu[...] = jnp.zeros_like(acc_gu)
    acc_b[...] = jnp.zeros_like(acc_b)
    for i in range(1, 4):
        yy = lax.rem(yl + 4 - i, 4)
        blk = G.at[z, :, yy]
        copy(blk, blk, y_ss.at[i], y_rs.at[i], at_y(yy)).wait_recv()

    def right(k, a):
        blk = G.at[lax.rem(z + NZ - k, NZ), a]
        return copy(blk, blk, r_ss.at[k, a], r_rs.at[k, a], at_z(lax.rem(z + 1, NZ)))

    def right_got(k, a):
        blk = G.at[lax.rem(z + NZ - 1 - k, NZ), a]
        return copy(blk, blk, r_ss.at[k, a], r_rs.at[k, a], at_z(lax.rem(z + 1, NZ)))

    def left(k, a):
        blk = G.at[lax.rem(z + k, NZ), a]
        return copy(blk, blk, l_ss.at[k, a], l_rs.at[k, a], at_z(lax.rem(z + NZ - 1, NZ)))

    def left_got(k, a):
        blk = G.at[lax.rem(z + k + 1, NZ), a]
        return copy(blk, blk, l_ss.at[k, a], l_rs.at[k, a], at_z(lax.rem(z + NZ - 1, NZ)))

    def slot_of(n):
        if n == 0:
            return z
        if n <= 3:
            return lax.rem(z + NZ - n, NZ)
        if n <= 6:
            return lax.rem(z + n - 3, NZ)
        return lax.rem(z + 4, NZ)

    def products(slot):
        base = pl.multiple_of(slot * FEAT, FEAT)
        rows_in = G[slot, 0].reshape(HALF, FEAT)
        rows_back = G[slot, 1].reshape(HALF, FEAT)
        acc_gu[...] += jnp.dot(
            rows_in, wgu[pl.ds(base, FEAT), :], preferred_element_type=jnp.float32
        )
        acc_b[...] += lax.dot_general(
            rows_back, wdn[:, pl.ds(base, FEAT)], (((1,), (1,)), ((), ())),
            preferred_element_type=jnp.float32,
        )

    for a in range(2):
        start(right(0, a))
        start(left(0, a))
    for ld in loads:
        ld.wait()
    for i, (src, dst) in enumerate(weights(1 - c)):
        copy(src, dst, p_ss.at[i], p_rs.at[i], sibling).wait_recv()
    products(z)
    for k in range(3):
        for a in range(2):
            right_got(k, a).wait_recv()
            if k < 2 or a == 0:
                start(right(k + 1, a))
            left_got(k, a).wait_recv()
            if k < 2 or a == 1:
                start(left(k + 1, a))
        products(slot_of(k + 1))
        products(slot_of(k + 4))
    right_got(3, 0).wait_recv()
    left_got(3, 1).wait_recv()
    products(slot_of(7))

    gate = acc_gu[:, : 2 * HID]
    up = acc_gu[:, 2 * HID :]
    bg = acc_b[...]
    sg = jax.nn.sigmoid(gate)
    silu = gate * sg
    gcat[:, : 2 * HID] = (bg * up * sg * (1.0 + gate * (1.0 - sg))).astype(jnp.bfloat16)
    gcat[:, 2 * HID :] = (bg * silu).astype(jnp.bfloat16)
    score = jnp.sum(silu * up * bg, axis=1, keepdims=True)

    def slice_grad(slot):
        base = pl.multiple_of(slot * FEAT, FEAT)
        part[slot] = lax.dot_general(
            gcat[...], wgu[pl.ds(base, FEAT), :], (((1,), (1,)), ((), ())),
            preferred_element_type=jnp.float32,
        )

    def ring_r(k):
        rows = pl.ds(0, SUB) if k == 0 else pl.ds(0, HALF)
        return copy(
            rsend.at[k, rows], rrecv.at[k, rows], rr_ss.at[k], rr_rs.at[k],
            at_z(lax.rem(z + 1, NZ)),
        )

    def ring_l(k):
        rows = pl.ds(SUB, SUB) if k == 0 else pl.ds(0, HALF)
        return copy(
            lsend.at[k, rows], lrecv.at[k, rows], rl_ss.at[k], rl_rs.at[k],
            at_z(lax.rem(z + NZ - 1, NZ)),
        )

    slice_grad(slot_of(7))
    rsend[0, :SUB] = part[slot_of(7), :SUB].astype(jnp.bfloat16)
    start(ring_r(0))
    lsend[0, SUB:] = part[slot_of(7), SUB:].astype(jnp.bfloat16)
    start(ring_l(0))

    q = iota((HALF, 128), 0)
    for v in (2, 1):
        q = jnp.where(q >= v * BLK, q - v * BLK, q)
    j6 = div6(q)
    spread = jnp.where(iota((HALF, 128), 1) == j6 * 8 + (q - 6 * j6), score, 0.0)
    g = iota((8, HALF), 0)
    n = iota((8, HALF), 1)
    mine = ((n >= g * BLK) & (n < g * BLK + BLK)).astype(jnp.float32)
    scz[z] = jnp.dot(mine, spread, precision=HIGH, preferred_element_type=jnp.float32)
    for i in range(1, NZ):
        start(copy(scz.at[z], scz.at[z], z_ss.at[i], z_rs.at[i], at_z(lax.rem(z + i, NZ))))

    for k in range(1, 4):
        nr, nl = slot_of(7 - k), slot_of(4 - k)
        slice_grad(nr)
        slice_grad(nl)
        ring_r(k - 1).wait_recv()
        if k == 1:
            rsend[1, SUB:] = part[nr, SUB:].astype(jnp.bfloat16)
            rsend[1, :SUB] = (part[nr, :SUB] + rrecv[0, :SUB].astype(jnp.float32)).astype(
                jnp.bfloat16
            )
        else:
            rsend[k] = (part[nr] + rrecv[k - 1].astype(jnp.float32)).astype(jnp.bfloat16)
        start(ring_r(k))
        ring_l(k - 1).wait_recv()
        if k == 1:
            lsend[1, :SUB] = part[nl, :SUB].astype(jnp.bfloat16)
            lsend[1, SUB:] = (part[nl, SUB:] + lrecv[0, SUB:].astype(jnp.float32)).astype(
                jnp.bfloat16
            )
        else:
            lsend[k] = (part[nl] + lrecv[k - 1].astype(jnp.float32)).astype(jnp.bfloat16)
        start(ring_l(k))
        if k == 2:
            for i in range(1, NZ):
                zz = lax.rem(z + NZ - i, NZ)
                copy(scz.at[zz], scz.at[zz], z_ss.at[i], z_rs.at[i], at_z(zz)).wait_recv()
            scy[yl] = jnp.sum(scz[...], axis=0)
            for i in range(1, 4):
                yy = lax.rem(yl + i, 4)
                start(copy(scy.at[yl], scy.at[yl], s_ss.at[i], s_rs.at[i], at_y(yy)))
    slice_grad(z)
    for i in range(1, 4):
        yy = lax.rem(yl + 4 - i, 4)
        copy(scy.at[yy], scy.at[yy], s_ss.at[i], s_rs.at[i], at_y(yy)).wait_recv()
    scs[...] = jnp.sum(scy[...], axis=0)
    ring_r(3).wait_recv()
    ring_l(3).wait_recv()
    summed = part[z] + rrecv[3].astype(jnp.float32) + lrecv[3].astype(jnp.float32)
    total[...] = summed.reshape(4, BLK, FEAT)
    ysend[...] = summed.astype(jnp.bfloat16).reshape(4, BLK, FEAT)
    for i in range(1, 4):
        yy = lax.rem(yl + i, 4)
        start(copy(ysend.at[yy], yrecv.at[i], yy_ss.at[i], yy_rs.at[i], at_y(yy)))
    rows = total[yl]
    for i in range(1, 4):
        copy(ysend.at[0], yrecv.at[i], yy_ss.at[i], yy_rs.at[i], at_y(yl)).wait_recv()
        rows = rows + yrecv[i].astype(jnp.float32)

    r = iota((64, BLK), 0)
    pos = iota((64, BLK), 1)
    sel = (((r & 7) < CAP) & (pos == (r >> 3) * 6 + (r & 7))).astype(jnp.float32)
    ret[:, :, :FEAT] = jnp.dot(
        sel, rows, precision=HIGH, preferred_element_type=jnp.float32
    ).reshape(EXPERTS, 8, FEAT)
    ret[:, :, FEAT:] = jnp.broadcast_to(scs[...][None], (EXPERTS, 8, 128))
    for i in range(1, 8):
        e = lax.rem(own + i, 8)
        start(copy(ret.at[e], back.at[own], t_ss.at[i], t_rs.at[i], at_expert(e)))
    back[own] = ret[own]
    r = iota((64, TOK), 0)
    hits = []
    weight = jnp.zeros((64, TOK), jnp.float32)
    for k in range(2):
        hit = (ids[k : k + 1, :] == (r >> 3)) & (slots[k : k + 1, :] == (r & 7))
        hits.append(hit)
        weight = weight + jnp.where(hit, gates[k : k + 1, :], 0.0)
    for i in range(1, 8):
        j = lax.rem(own + 8 - i, 8)
        copy(ret.at[j], back.at[j], t_ss.at[i], t_rs.at[i], at_expert(j)).wait_recv()
    d_tok[...] = lax.dot_general(
        weight, back[:, :, :FEAT].reshape(64, FEAT), (((0,), (0,)), ((), ())),
        precision=HIGH, preferred_element_type=jnp.float32,
    ).astype(jnp.bfloat16)
    sc = back[:, :, FEAT:]
    same = lax.rem(iota((EXPERTS, 8, 128), 0) + own, 2) == 0
    row = jnp.where(same, yl, 3 - yl)
    sc = jnp.sum(jnp.where(iota((EXPERTS, 8, 128), 1) == row, sc, 0.0), axis=1, keepdims=True)
    sc = jnp.broadcast_to(sc, (EXPERTS, 8, 128)).reshape(64, 128)
    lane = own * 8 + (iota((64, 128), 0) & 7)
    sc = jnp.sum(jnp.where(iota((64, 128), 1) == lane, sc, 0.0), axis=1, keepdims=True)
    for k in range(2):
        d_gate[k : k + 1, :] = jnp.sum(jnp.where(hits[k], sc, 0.0), axis=0, keepdims=True)
    for cp in waits:
        cp.wait_send()


def local(tokens_in, d_out, gates, expert_ids, slot_ids, w_gate, w_up, w_down):
    vmem = pl.BlockSpec(memory_space=pltpu.VMEM)
    hbm = pl.BlockSpec(memory_space=pltpu.HBM)
    bf, f32, dma = jnp.bfloat16, jnp.float32, pltpu.SemaphoreType.DMA
    scratch = [
        pltpu.VMEM((TOK, FEAT), bf),
        pltpu.VMEM((TOK, FEAT), bf),
        pltpu.VMEM((2, TOK), f32),
        pltpu.VMEM((2, TOK), jnp.int32),
        pltpu.VMEM((2, TOK), jnp.int32),
        pltpu.VMEM((NZ * FEAT, 4 * HID), bf),
        pltpu.VMEM((2 * HID, NZ * FEAT), bf),
        pltpu.VMEM((EXPERTS, 16, FEAT), bf),
        pltpu.VMEM((EXPERTS, 16, FEAT), bf),
        pltpu.VMEM((NZ, 2, 4, BLK, FEAT), bf),
        pltpu.VMEM((HALF, 4 * HID), f32),
        pltpu.VMEM((HALF, 2 * HID), f32),
        pltpu.VMEM((HALF, 4 * HID), bf),
        pltpu.VMEM((NZ, HALF, FEAT), f32),
        pltpu.VMEM((4, HALF, FEAT), bf),
        pltpu.VMEM((4, HALF, FEAT), bf),
        pltpu.VMEM((4, HALF, FEAT), bf),
        pltpu.VMEM((4, HALF, FEAT), bf),
        pltpu.VMEM((4, BLK, FEAT), f32),
        pltpu.VMEM((4, BLK, FEAT), bf),
        pltpu.VMEM((4, BLK, FEAT), bf),
        pltpu.VMEM((EXPERTS, 8, FEAT + 128), f32),
        pltpu.VMEM((EXPERTS, 8, FEAT + 128), f32),
        pltpu.VMEM((NZ, 8, 128), f32),
        pltpu.VMEM((4, 8, 128), f32),
        pltpu.VMEM((8, 128), f32),
        dma((5,)), dma((3,)),
        dma((3,)), dma((3,)),
        dma((8,)), dma((8,)),
        dma((4,)), dma((4,)),
        dma((4, 2)), dma((4, 2)),
        dma((4, 2)), dma((4, 2)),
        dma((4,)), dma((4,)),
        dma((4,)), dma((4,)),
        dma((4,)), dma((4,)),
        dma((8,)), dma((8,)),
        dma((8,)), dma((8,)),
        dma((4,)), dma((4,)),
    ]
    d_tok, d_gate = pl.pallas_call(
        kernel,
        out_shape=(
            jax.ShapeDtypeStruct((TOK, FEAT), bf),
            jax.ShapeDtypeStruct((2, TOK), f32),
        ),
        in_specs=[hbm] * 8,
        out_specs=(vmem, vmem),
        scratch_shapes=scratch,
        name="moe_dx",
        compiler_params=pltpu.CompilerParams(
            collective_id=0, has_side_effects=True, vmem_limit_bytes=60 * 2**20
        ),
        cost_estimate=pl.CostEstimate(
            flops=5 * 2 * HALF * NZ * FEAT * 2 * HID, bytes_accessed=6 * NZ * FEAT * HID, transcendentals=HALF * 2 * HID
        ),
    )(tokens_in, d_out, gates.T, expert_ids.T, slot_ids.T, w_gate, w_up, w_down)
    return d_tok, d_gate.T


def solution(mesh):
    placed = (
        P("ep", "tp"),
        P("ep", "tp"),
        P("ep", None),
        P("ep", None),
        P("ep", None),
        P(None, ("ep", "tp")),
        P(None, ("ep", "tp")),
        P(("ep", "tp"), None),
    )
    return jax.shard_map(
        local, mesh=mesh, in_specs=placed, out_specs=(P("ep", "tp"), P("ep", None)), check_vma=False
    )
```

time: 102 us -> 90 us (0.88)
  the two profiles are of different devices: /device:TPU:16 before, /device:TPU:8 now
where the time goes in v2:
time: 90 us; the launch traced here: 89.8 us
  Pallas kernels  86.6 us (96%)
  local copies, waits for them, and re-layouts  2.52 us (3%)
    pallas_call x1, Pallas kernels, local(): pl.pallas_call(kernel, out_shape=(jax.ShapeDtypeStruct((TOK, FEAT), bf),...  86.6 us
    unnamed x2, local copies, waits for them, and re-layouts  2.52 us

profile of v2, /device:TPU:8, one launch (start us, length us, event | category | flops | bytes accessed | tf_op | source)
XLA Modules:
  0.0 89.8 jit_solution(1247321197502996783)
XLA Ops:
  0.6 86.6 %moe_dx.1 = (bf16[16,384]{1,0:T(8,128)(2,1)}, f32[2,16]{1,0:T(2,128)}) custom-call(bf16[16,384]{1,0:T(8,128)(2,1)} %tok_h.1, bf16[16,384]{1,0:T(8,128)(2,1)} %dout_h.1, f32[2,16]{1,0:T(2,128)} %bitcast.5, s32[2,16]{1,0:T(2,128)} %bitcast.6, s32[2,16]{1,0:T(2,128)} %bitcast.7, bf16[3072,256]{1,0:T(8,128)(2,1)} %wg.1, bf16[3072,256]{1,0:T(8,128)(2,1)} %wu.1, ...), custom_call_target="tpu_custom_call" | custom-call | flops 3019898880 | bytes 4718592 | tf_op jit(solution)/shard_map/moe_dx/pallas_call | solution.py:377
  87.2 1.3 %copy.12 = bf16[16,384]{1,0:T(8,128)(2,1)} copy(bf16[16,384]{1,0:T(8,128)(2,1)} %get-tuple-element.8) | data formatting | bytes 24576
  88.5 1.2 %copy.13 = f32[16,2]{0,1:T(2,128)} copy(f32[16,2]{0,1:T(2,128)} %bitcast.4) | data formatting | bytes 256

commit v3 on v2

--- a/solution.py
+++ b/solution.py
@@ -15,7 +15,9 @@
 HID = 256
 BLK = 48
 HALF = 192
-SUB = HALF // 2
+PR = 32
+QR = BLK - PR
+PALL = 4 * PR
 
 
 def iota(shape, dim):
@@ -24,13 +26,19 @@
 
 def div6(v):
     return (v * 43) >> 8
+
+
+def row_of(r):
+    q = r - PALL
+    first = r < PALL
+    return jnp.where(first, r >> 5, q >> 4), jnp.where(first, r & (PR - 1), PR + (q & (QR - 1)))
 
 
 def kernel(
     tok_h, dout_h, gates_h, ids_h, slots_h, wg, wu, wd, d_tok, d_gate,
     tok, dout, gates, ids, slots, wgu, wdn, send, drecv, G, acc_gu, acc_b, gcat, part,
     rsend, rrecv, lsend, lrecv, total, ysend, yrecv, ret, back, scz, scy, scs,
-    i_sem, w_sem, p_ss, p_rs, d_ss, d_rs, y_ss, y_rs, r_ss, r_rs, l_ss, l_rs,
+    i_sem, w_sem, p_ss, p_rs, d_ss, d_rs, y_ss, y_rs, q_ss, q_rs, qz_ss, qz_rs, r_ss, r_rs, l_ss, l_rs,
     rr_ss, rr_rs, rl_ss, rl_rs, yy_ss, yy_rs, t_ss, t_rs, z_ss, z_rs, s_ss, s_rs,
 ):
     ep = lax.axis_index("ep")
@@ -123,35 +131,11 @@
         copy(send.at[j], drecv.at[j], d_ss.at[i], d_rs.at[i], at_expert(j)).wait_recv()
     dense = jnp.dot(sel, drecv[...].reshape(128, FEAT), preferred_element_type=jnp.float32)
     dense = dense.astype(jnp.bfloat16)
-    G[z, 0, yl] = dense[:BLK]
-    G[z, 1, yl] = dense[BLK:]
-
-    for i in range(1, 4):
-        yy = lax.rem(yl + i, 4)
-        blk = G.at[z, :, yl]
-        start(copy(blk, blk, y_ss.at[i], y_rs.at[i], at_y(yy)))
-    acc_gu[...] = jnp.zeros_like(acc_gu)
-    acc_b[...] = jnp.zeros_like(acc_b)
-    for i in range(1, 4):
-        yy = lax.rem(yl + 4 - i, 4)
-        blk = G.at[z, :, yy]
-        copy(blk, blk, y_ss.at[i], y_rs.at[i], at_y(yy)).wait_recv()
-
-    def right(k, a):
-        blk = G.at[lax.rem(z + NZ - k, NZ), a]
-        return copy(blk, blk, r_ss.at[k, a], r_rs.at[k, a], at_z(lax.rem(z + 1, NZ)))
-
-    def right_got(k, a):
-        blk = G.at[lax.rem(z + NZ - 1 - k, NZ), a]
-        return copy(blk, blk, r_ss.at[k, a], r_rs.at[k, a], at_z(lax.rem(z + 1, NZ)))
-
-    def left(k, a):
-        blk = G.at[lax.rem(z + k, NZ), a]
-        return copy(blk, blk, l_ss.at[k, a], l_rs.at[k, a], at_z(lax.rem(z + NZ - 1, NZ)))
-
-    def left_got(k, a):
-        blk = G.at[lax.rem(z + k + 1, NZ), a]
-        return copy(blk, blk, l_ss.at[k, a], l_rs.at[k, a], at_z(lax.rem(z + NZ - 1, NZ)))
+    p_rows = pl.ds(pl.multiple_of(yl * PR, PR), PR)
+    q_rows = pl.ds(pl.multiple_of(PALL + yl * QR, QR), QR)
+    for a in range(2):
+        G[z, a, p_rows, :] = dense[a * BLK : a * BLK + PR]
+        G[z, a, q_rows, :] = dense[a * BLK + PR : (a + 1) * BLK]
 
     def slot_of(n):
         if n == 0:
@@ -162,110 +146,162 @@
             return lax.rem(z + n - 3, NZ)
         return lax.rem(z + 4, NZ)
 
-    def products(slot):
+    z_right, z_left = at_z(lax.rem(z + 1, NZ)), at_z(lax.rem(z + NZ - 1, NZ))
+
+    def q_own(i):
+        blk = G.at[z, :, q_rows]
+        return copy(blk, blk, qz_ss.at[i], qz_rs.at[i], at_z(lax.rem(z + i, NZ)))
+
+    def q_from(i):
+        zz = lax.rem(z + NZ - i, NZ)
+        blk = G.at[zz, :, q_rows]
+        return copy(blk, blk, qz_ss.at[i], qz_rs.at[i], at_z(zz))
+
+    def q_spread(n):
+        blk = G.at[slot_of(n), :, q_rows]
+        for i in range(1, 4):
+            start(copy(blk, blk, q_ss.at[n, i], q_rs.at[n, i], at_y(lax.rem(yl + i, 4))))
+
+    def q_got(n):
+        for i in range(1, 4):
+            yy = lax.rem(yl + 4 - i, 4)
+            blk = G.at[slot_of(n), :, pl.ds(pl.multiple_of(PALL + yy * QR, QR), QR)]
+            copy(blk, blk, q_ss.at[n, i], q_rs.at[n, i], at_y(yy)).wait_recv()
+
+    def over_y(i, yy, dev):
+        blk = G.at[z, :, pl.ds(pl.multiple_of(yy * PR, PR), PR)]
+        return copy(blk, blk, y_ss.at[i], y_rs.at[i], dev)
+
+    def right(k, a, shift=0):
+        blk = G.at[lax.rem(z + NZ - k - shift, NZ), a, pl.ds(0, PALL)]
+        return copy(blk, blk, r_ss.at[k, a], r_rs.at[k, a], z_right)
+
+    def left(k, a, shift=0):
+        blk = G.at[lax.rem(z + k + shift, NZ), a, pl.ds(0, PALL)]
+        return copy(blk, blk, l_ss.at[k, a], l_rs.at[k, a], z_left)
+
+    def p_step(k):
+        for a in range(2):
+            if k < 3 or a == 0:
+                right(k, a, 1).wait_recv()
+                if k < 2 or (k == 2 and a == 0):
+                    start(right(k + 1, a))
+            if k < 3 or a == 1:
+                left(k, a, 1).wait_recv()
+                if k < 2 or (k == 2 and a == 1):
+                    start(left(k + 1, a))
+
+    def products(n):
+        q_got(n)
+        slot = slot_of(n)
         base = pl.multiple_of(slot * FEAT, FEAT)
-        rows_in = G[slot, 0].reshape(HALF, FEAT)
-        rows_back = G[slot, 1].reshape(HALF, FEAT)
         acc_gu[...] += jnp.dot(
-            rows_in, wgu[pl.ds(base, FEAT), :], preferred_element_type=jnp.float32
+            G[slot, 0], wgu[pl.ds(base, FEAT), :], preferred_element_type=jnp.float32
         )
         acc_b[...] += lax.dot_general(
-            rows_back, wdn[:, pl.ds(base, FEAT)], (((1,), (1,)), ((), ())),
+            G[slot, 1], wdn[:, pl.ds(base, FEAT)], (((1,), (1,)), ((), ())),
             preferred_element_type=jnp.float32,
         )
 
+    near = (1, 7, 2, 6, 3, 5, 4)
+    for i in near:
+        start(q_own(i))
+    for i in range(1, 4):
+        yy = lax.rem(yl + i, 4)
+        start(over_y(i, yl, at_y(yy)))
+    q_spread(0)
+    acc_gu[...] = jnp.zeros_like(acc_gu)
+    acc_b[...] = jnp.zeros_like(acc_b)
+    for i in range(1, 4):
+        yy = lax.rem(yl + 4 - i, 4)
+        over_y(i, yy, at_y(yy)).wait_recv()
     for a in range(2):
         start(right(0, a))
         start(left(0, a))
+    for i in near:
+        q_from(i).wait_recv()
+        q_spread(i if i <= 3 else 7 if i == 4 else 11 - i)
     for ld in loads:
         ld.wait()
     for i, (src, dst) in enumerate(weights(1 - c)):
         copy(src, dst, p_ss.at[i], p_rs.at[i], sibling).wait_recv()
-    products(z)
-    for k in range(3):
-        for a in range(2):
-            right_got(k, a).wait_recv()
-            if k < 2 or a == 0:
-                start(right(k + 1, a))
-            left_got(k, a).wait_recv()
-            if k < 2 or a == 1:
-                start(left(k + 1, a))
-        products(slot_of(k + 1))
-        products(slot_of(k + 4))
-    right_got(3, 0).wait_recv()
-    left_got(3, 1).wait_recv()
-    products(slot_of(7))
-
-    gate = acc_gu[:, : 2 * HID]
-    up = acc_gu[:, 2 * HID :]
-    bg = acc_b[...]
-    sg = jax.nn.sigmoid(gate)
-    silu = gate * sg
-    gcat[:, : 2 * HID] = (bg * up * sg * (1.0 + gate * (1.0 - sg))).astype(jnp.bfloat16)
-    gcat[:, 2 * HID :] = (bg * silu).astype(jnp.bfloat16)
-    score = jnp.sum(silu * up * bg, axis=1, keepdims=True)
-
-    def slice_grad(slot):
+    p_step(0)
+    products(0)
+    p_step(1)
+    products(1)
+    products(4)
+    p_step(2)
+    products(2)
+    products(5)
+    products(3)
+    products(6)
+    p_step(3)
+    products(7)
+
+    parts = (pl.ds(0, PALL), pl.ds(PALL, HALF - PALL))
+
+    def hidden(h):
+        gate = acc_gu[parts[h], : 2 * HID]
+        up = acc_gu[parts[h], 2 * HID :]
+        bg = acc_b[parts[h], :]
+        sg = jax.nn.sigmoid(gate)
+        silu = gate * sg
+        gcat[parts[h], : 2 * HID] = (bg * up * sg * (1.0 + gate * (1.0 - sg))).astype(jnp.bfloat16)
+        gcat[parts[h], 2 * HID :] = (bg * silu).astype(jnp.bfloat16)
+        return jnp.sum(silu * up * bg, axis=1, keepdims=True)
+
+    def slice_grad(slot, rows):
         base = pl.multiple_of(slot * FEAT, FEAT)
-        part[slot] = lax.dot_general(
-            gcat[...], wgu[pl.ds(base, FEAT), :], (((1,), (1,)), ((), ())),
+        part[slot, rows, :] = lax.dot_general(
+            gcat[rows, :], wgu[pl.ds(base, FEAT), :], (((1,), (1,)), ((), ())),
             preferred_element_type=jnp.float32,
         )
 
-    def ring_r(k):
-        rows = pl.ds(0, SUB) if k == 0 else pl.ds(0, HALF)
+    def ring_r(k, h):
         return copy(
-            rsend.at[k, rows], rrecv.at[k, rows], rr_ss.at[k], rr_rs.at[k],
-            at_z(lax.rem(z + 1, NZ)),
-        )
-
-    def ring_l(k):
-        rows = pl.ds(SUB, SUB) if k == 0 else pl.ds(0, HALF)
+            rsend.at[k, parts[h]], rrecv.at[k, parts[h]], rr_ss.at[k, h], rr_rs.at[k, h], z_right
+        )
+
+    def ring_l(k, h):
         return copy(
-            lsend.at[k, rows], lrecv.at[k, rows], rl_ss.at[k], rl_rs.at[k],
-            at_z(lax.rem(z + NZ - 1, NZ)),
-        )
-
-    slice_grad(slot_of(7))
-    rsend[0, :SUB] = part[slot_of(7), :SUB].astype(jnp.bfloat16)
-    start(ring_r(0))
-    lsend[0, SUB:] = part[slot_of(7), SUB:].astype(jnp.bfloat16)
-    start(ring_l(0))
-
-    q = iota((HALF, 128), 0)
-    for v in (2, 1):
-        q = jnp.where(q >= v * BLK, q - v * BLK, q)
+            lsend.at[k, parts[h]], lrecv.at[k, parts[h]], rl_ss.at[k, h], rl_rs.at[k, h], z_left
+        )
+
+    far = slot_of(7)
+    score0 = hidden(0)
+    slice_grad(far, parts[0])
+    rsend[0, parts[0], :] = part[far, parts[0], :].astype(jnp.bfloat16)
+    start(ring_r(0, 0))
+    score1 = hidden(1)
+    slice_grad(far, parts[1])
+    lsend[0, parts[1], :] = part[far, parts[1], :].astype(jnp.bfloat16)
+    start(ring_l(0, 1))
+    score = jnp.concatenate([score0, score1], axis=0)
+
+    q = row_of(iota((HALF, 128), 0))[1]
     j6 = div6(q)
     spread = jnp.where(iota((HALF, 128), 1) == j6 * 8 + (q - 6 * j6), score, 0.0)
-    g = iota((8, HALF), 0)
-    n = iota((8, HALF), 1)
-    mine = ((n >= g * BLK) & (n < g * BLK + BLK)).astype(jnp.float32)
+    mine = (row_of(iota((8, HALF), 1))[0] == iota((8, HALF), 0)).astype(jnp.float32)
     scz[z] = jnp.dot(mine, spread, precision=HIGH, preferred_element_type=jnp.float32)
     for i in range(1, NZ):
         start(copy(scz.at[z], scz.at[z], z_ss.at[i], z_rs.at[i], at_z(lax.rem(z + i, NZ))))
 
     for k in range(1, 4):
         nr, nl = slot_of(7 - k), slot_of(4 - k)
-        slice_grad(nr)
-        slice_grad(nl)
-        ring_r(k - 1).wait_recv()
-        if k == 1:
-            rsend[1, SUB:] = part[nr, SUB:].astype(jnp.bfloat16)
-            rsend[1, :SUB] = (part[nr, :SUB] + rrecv[0, :SUB].astype(jnp.float32)).astype(
-                jnp.bfloat16
-            )
-        else:
-            rsend[k] = (part[nr] + rrecv[k - 1].astype(jnp.float32)).astype(jnp.bfloat16)
-        start(ring_r(k))
-        ring_l(k - 1).wait_recv()
-        if k == 1:
-            lsend[1, :SUB] = part[nl, :SUB].astype(jnp.bfloat16)
-            lsend[1, SUB:] = (part[nl, SUB:] + lrecv[0, SUB:].astype(jnp.float32)).astype(
-                jnp.bfloat16
-            )
-        else:
-            lsend[k] = (part[nl] + lrecv[k - 1].astype(jnp.float32)).astype(jnp.bfloat16)
-        start(ring_l(k))
+        slice_grad(nr, pl.ds(0, HALF))
+        slice_grad(nl, pl.ds(0, HALF))
+        for h, ring, slot, out, got in (
+            (1, ring_r, nr, rsend, rrecv),
+            (0, ring_l, nl, lsend, lrecv),
+            (0, ring_r, nr, rsend, rrecv),
+            (1, ring_l, nl, lsend, lrecv),
+        ):
+            term = part[slot, parts[h], :]
+            if k > 1 or (h == 0) == (out is rsend):
+                ring(k - 1, h).wait_recv()
+                term = term + got[k - 1, parts[h], :].astype(jnp.float32)
+            out[k, parts[h], :] = term.astype(jnp.bfloat16)
+            start(ring(k, h))
         if k == 2:
             for i in range(1, NZ):
                 zz = lax.rem(z + NZ - i, NZ)
@@ -274,22 +310,32 @@
             for i in range(1, 4):
                 yy = lax.rem(yl + i, 4)
                 start(copy(scy.at[yl], scy.at[yl], s_ss.at[i], s_rs.at[i], at_y(yy)))
-    slice_grad(z)
+    slice_grad(z, pl.ds(0, HALF))
     for i in range(1, 4):
         yy = lax.rem(yl + 4 - i, 4)
         copy(scy.at[yy], scy.at[yy], s_ss.at[i], s_rs.at[i], at_y(yy)).wait_recv()
     scs[...] = jnp.sum(scy[...], axis=0)
-    ring_r(3).wait_recv()
-    ring_l(3).wait_recv()
-    summed = part[z] + rrecv[3].astype(jnp.float32) + lrecv[3].astype(jnp.float32)
-    total[...] = summed.reshape(4, BLK, FEAT)
-    ysend[...] = summed.astype(jnp.bfloat16).reshape(4, BLK, FEAT)
+    places = (pl.ds(0, PR), pl.ds(PR, QR))
+    for h, size in ((1, QR), (0, PR)):
+        ring_r(3, h).wait_recv()
+        ring_l(3, h).wait_recv()
+        summed = part[z, parts[h], :] + rrecv[3, parts[h], :].astype(jnp.float32)
+        summed = summed + lrecv[3, parts[h], :].astype(jnp.float32)
+        total[parts[h], :] = summed
+        ysend[:, places[h], :] = summed.astype(jnp.bfloat16).reshape(4, size, FEAT)
+        for i in range(1, 4):
+            yy = lax.rem(yl + i, 4)
+            start(
+                copy(
+                    ysend.at[yy, places[h]], yrecv.at[i, places[h]],
+                    yy_ss.at[i, h], yy_rs.at[i, h], at_y(yy),
+                )
+            )
+    rows = jnp.concatenate([total[p_rows, :], total[q_rows, :]], axis=0)
     for i in range(1, 4):
-        yy = lax.rem(yl + i, 4)
-        start(copy(ysend.at[yy], yrecv.at[i], yy_ss.at[i], yy_rs.at[i], at_y(yy)))
-    rows = total[yl]
-    for i in range(1, 4):
-        copy(ysend.at[0], yrecv.at[i], yy_ss.at[i], yy_rs.at[i], at_y(yl)).wait_recv()
+        for h in (1, 0):
+            dst = yrecv.at[i, places[h]]
+            copy(dst, dst, yy_ss.at[i, h], yy_rs.at[i, h], at_y(lax.rem(yl + 4 - i, 4))).wait_recv()
         rows = rows + yrecv[i].astype(jnp.float32)
 
     r = iota((64, BLK), 0)
@@ -344,7 +390,7 @@
         pltpu.VMEM((2 * HID, NZ * FEAT), bf),
         pltpu.VMEM((EXPERTS, 16, FEAT), bf),
         pltpu.VMEM((EXPERTS, 16, FEAT), bf),
-        pltpu.VMEM((NZ, 2, 4, BLK, FEAT), bf),
+        pltpu.VMEM((NZ, 2, HALF, FEAT), bf),
         pltpu.VMEM((HALF, 4 * HID), f32),
         pltpu.VMEM((HALF, 2 * HID), f32),
         pltpu.VMEM((HALF, 4 * HID), bf),
@@ -353,7 +399,7 @@
         pltpu.VMEM((4, HALF, FEAT), bf),
         pltpu.VMEM((4, HALF, FEAT), bf),
         pltpu.VMEM((4, HALF, FEAT), bf),
-        pltpu.VMEM((4, BLK, FEAT), f32),
+        pltpu.VMEM((HALF, FEAT), f32),
         pltpu.VMEM((4, BLK, FEAT), bf),
         pltpu.VMEM((4, BLK, FEAT), bf),
         pltpu.VMEM((EXPERTS, 8, FEAT + 128), f32),
@@ -365,11 +411,13 @@
         dma((3,)), dma((3,)),
         dma((8,)), dma((8,)),
         dma((4,)), dma((4,)),
+        dma((8, 4)), dma((8, 4)),
+        dma((8,)), dma((8,)),
         dma((4, 2)), dma((4, 2)),
         dma((4, 2)), dma((4, 2)),
-        dma((4,)), dma((4,)),
-        dma((4,)), dma((4,)),
-        dma((4,)), dma((4,)),
+        dma((4, 2)), dma((4, 2)),
+        dma((4, 2)), dma((4, 2)),
+        dma((4, 2)), dma((4, 2)),
         dma((8,)), dma((8,)),
         dma((8,)), dma((8,)),
         dma((4,)), dma((4,)),

time: 90 us -> 82.1 us (0.912)
  Pallas kernels: 86.6 us -> 78.7 us
    pallas_call x1, Pallas kernels: 86.6 us -> 78.7 us  [local(): pl.pallas_call(kernel, out_shape=(jax.ShapeDtypeStruct((TOK, FEAT), bf),...]
where the time goes in v3:
time: 82.1 us; the launch traced here: 81.9 us
  Pallas kernels  78.7 us (96%)
  local copies, waits for them, and re-layouts  2.52 us (3%)
    pallas_call x1, Pallas kernels, local(): pl.pallas_call(kernel, out_shape=(jax.ShapeDtypeStruct((TOK, FEAT), bf),...  78.7 us
    unnamed x2, local copies, waits for them, and re-layouts  2.52 us

profile of v3, /device:TPU:8, one launch (start us, length us, event | category | flops | bytes accessed | tf_op | source)
XLA Modules:
  0.0 81.9 jit_solution(10500430327777159651)
XLA Ops:
  0.6 78.7 %moe_dx.1 = (bf16[16,384]{1,0:T(8,128)(2,1)}, f32[2,16]{1,0:T(2,128)}) custom-call(bf16[16,384]{1,0:T(8,128)(2,1)} %tok_h.1, bf16[16,384]{1,0:T(8,128)(2,1)} %dout_h.1, f32[2,16]{1,0:T(2,128)} %bitcast.5, s32[2,16]{1,0:T(2,128)} %bitcast.6, s32[2,16]{1,0:T(2,128)} %bitcast.7, bf16[3072,256]{1,0:T(8,128)(2,1)} %wg.1, bf16[3072,256]{1,0:T(8,128)(2,1)} %wu.1, ...), custom_call_target="tpu_custom_call" | custom-call | flops 3019898880 | bytes 4718592 | tf_op jit(solution)/shard_map/moe_dx/pallas_call | solution.py:425
  79.3 1.3 %copy.12 = bf16[16,384]{1,0:T(8,128)(2,1)} copy(bf16[16,384]{1,0:T(8,128)(2,1)} %get-tuple-element.8) | data formatting | bytes 24576
  80.6 1.2 %copy.13 = f32[16,2]{0,1:T(2,128)} copy(f32[16,2]{0,1:T(2,128)} %bitcast.4) | data formatting | bytes 256

commit v4 on v3

--- a/solution.py
+++ b/solution.py
@@ -50,13 +50,13 @@
 
     def at_expert(e):
         mirrored = lax.rem(own + e, 2)
-        return (e * 8 + (yl + mirrored * (3 - 2 * yl)) * 2 + c, z)
+        return (e * 8 + (yl + mirrored * (3 - 2 * yl)) * 2 + lax.rem(c + z, 2), z)
 
     def at_y(yy):
         return (own * 8 + yy * 2 + c, z)
 
     def at_z(zz):
-        return (ep, zz)
+        return (own * 8 + yl * 2 + lax.rem(c + z + zz, 2), zz)
 
     sibling = (own * 8 + yl * 2 + 1 - c, z)
 
@@ -120,7 +120,14 @@
         start(copy(send.at[e], drecv.at[own], d_ss.at[i], d_rs.at[i], at_expert(e)))
     for i, (src, dst) in enumerate(weights(c)):
         start(copy(src, dst, p_ss.at[i], p_rs.at[i], sibling))
-    drecv[own] = send[own]
+    @pl.when(lax.rem(z, 2) == 0)
+    def _():
+        drecv[own] = send[own]
+
+    @pl.when(lax.rem(z, 2) == 1)
+    def _():
+        copy(send.at[own], drecv.at[own], d_ss.at[0], d_rs.at[0], sibling).start()
+
     r = iota((2 * BLK, 128), 0)
     second = (r >= BLK).astype(jnp.int32)
     q = r - second * BLK
@@ -129,6 +136,11 @@
     for i in range(1, 8):
         j = lax.rem(own + 8 - i, 8)
         copy(send.at[j], drecv.at[j], d_ss.at[i], d_rs.at[i], at_expert(j)).wait_recv()
+
+    @pl.when(lax.rem(z, 2) == 1)
+    def _():
+        copy(send.at[own], drecv.at[own], d_ss.at[0], d_rs.at[0], sibling).wait()
+
     dense = jnp.dot(sel, drecv[...].reshape(128, FEAT), preferred_element_type=jnp.float32)
     dense = dense.astype(jnp.bfloat16)
     p_rows = pl.ds(pl.multiple_of(yl * PR, PR), PR)
@@ -348,7 +360,14 @@
     for i in range(1, 8):
         e = lax.rem(own + i, 8)
         start(copy(ret.at[e], back.at[own], t_ss.at[i], t_rs.at[i], at_expert(e)))
-    back[own] = ret[own]
+    @pl.when(lax.rem(z, 2) == 0)
+    def _():
+        back[own] = ret[own]
+
+    @pl.when(lax.rem(z, 2) == 1)
+    def _():
+        copy(ret.at[own], back.at[own], t_ss.at[0], t_rs.at[0], sibling).start()
+
     r = iota((64, TOK), 0)
     hits = []
     weight = jnp.zeros((64, TOK), jnp.float32)
@@ -359,6 +378,11 @@
     for i in range(1, 8):
         j = lax.rem(own + 8 - i, 8)
         copy(ret.at[j], back.at[j], t_ss.at[i], t_rs.at[i], at_expert(j)).wait_recv()
+
+    @pl.when(lax.rem(z, 2) == 1)
+    def _():
+        copy(ret.at[own], back.at[own], t_ss.at[0], t_rs.at[0], sibling).wait()
+
     d_tok[...] = lax.dot_general(
         weight, back[:, :, :FEAT].reshape(64, FEAT), (((0,), (0,)), ((), ())),
         precision=HIGH, preferred_element_type=jnp.float32,

time: 82.1 us -> 80.3 us (0.978)
  Pallas kernels: 78.7 us -> 76.9 us
    pallas_call x1, Pallas kernels: 78.7 us -> 76.9 us  [local(): pl.pallas_call(kernel, out_shape=(jax.ShapeDtypeStruct((TOK, FEAT), bf),...]
where the time goes in v4:
time: 80.3 us; the launch traced here: 80.1 us
  Pallas kernels  76.9 us (96%)
  local copies, waits for them, and re-layouts  2.52 us (3%)
    pallas_call x1, Pallas kernels, local(): pl.pallas_call(kernel, out_shape=(jax.ShapeDtypeStruct((TOK, FEAT), bf),...  76.9 us
    unnamed x2, local copies, waits for them, and re-layouts  2.52 us

profile of v4, /device:TPU:8, one launch (start us, length us, event | category | flops | bytes accessed | tf_op | source)
XLA Modules:
  0.0 80.1 jit_solution(2650980292516055432)
XLA Ops:
  0.6 76.9 %moe_dx.1 = (bf16[16,384]{1,0:T(8,128)(2,1)}, f32[2,16]{1,0:T(2,128)}) custom-call(bf16[16,384]{1,0:T(8,128)(2,1)} %tok_h.1, bf16[16,384]{1,0:T(8,128)(2,1)} %dout_h.1, f32[2,16]{1,0:T(2,128)} %bitcast.5, s32[2,16]{1,0:T(2,128)} %bitcast.6, s32[2,16]{1,0:T(2,128)} %bitcast.7, bf16[3072,256]{1,0:T(8,128)(2,1)} %wg.1, bf16[3072,256]{1,0:T(8,128)(2,1)} %wu.1, ...), custom_call_target="tpu_custom_call" | custom-call | flops 3019898880 | bytes 4718592 | tf_op jit(solution)/shard_map/moe_dx/pallas_call | solution.py:449
  77.6 1.3 %copy.12 = bf16[16,384]{1,0:T(8,128)(2,1)} copy(bf16[16,384]{1,0:T(8,128)(2,1)} %get-tuple-element.8) | data formatting | bytes 24576
  78.9 1.2 %copy.13 = f32[16,2]{0,1:T(2,128)} copy(f32[16,2]{0,1:T(2,128)} %bitcast.4) | data formatting | bytes 256

commit v5 on v4

--- a/solution.py
+++ b/solution.py
@@ -169,6 +169,10 @@
         blk = G.at[zz, :, q_rows]
         return copy(blk, blk, qz_ss.at[i], qz_rs.at[i], at_z(zz))
 
+    def q_relay(slot, a, dev):
+        blk = G.at[slot, a, q_rows]
+        return copy(blk, blk, qz_ss.at[4 * a], qz_rs.at[4 * a], dev)
+
     def q_spread(n):
         blk = G.at[slot_of(n), :, q_rows]
         for i in range(1, 4):
@@ -215,7 +219,7 @@
             preferred_element_type=jnp.float32,
         )
 
-    near = (1, 7, 2, 6, 3, 5, 4)
+    near = (1, 7, 2, 6, 3, 5)
     for i in near:
         start(q_own(i))
     for i in range(1, 4):
@@ -224,6 +228,7 @@
     q_spread(0)
     acc_gu[...] = jnp.zeros_like(acc_gu)
     acc_b[...] = jnp.zeros_like(acc_b)
+    ret[...] = jnp.zeros_like(ret)
     for i in range(1, 4):
         yy = lax.rem(yl + 4 - i, 4)
         over_y(i, yy, at_y(yy)).wait_recv()
@@ -231,14 +236,22 @@
         start(right(0, a))
         start(left(0, a))
     for i in near:
+        if i == 3:
+            p_step(0)
         q_from(i).wait_recv()
-        q_spread(i if i <= 3 else 7 if i == 4 else 11 - i)
+        if i == 3:
+            start(q_relay(lax.rem(z + NZ - 3, NZ), 0, z_right))
+        if i == 5:
+            start(q_relay(lax.rem(z + 3, NZ), 1, z_left))
+        q_spread(i if i <= 3 else 11 - i)
     for ld in loads:
         ld.wait()
     for i, (src, dst) in enumerate(weights(1 - c)):
         copy(src, dst, p_ss.at[i], p_rs.at[i], sibling).wait_recv()
-    p_step(0)
     products(0)
+    q_relay(slot_of(7), 0, z_right).wait_recv()
+    q_relay(slot_of(7), 1, z_left).wait_recv()
+    q_spread(7)
     p_step(1)
     products(1)
     products(4)
@@ -350,12 +363,8 @@
             copy(dst, dst, yy_ss.at[i, h], yy_rs.at[i, h], at_y(lax.rem(yl + 4 - i, 4))).wait_recv()
         rows = rows + yrecv[i].astype(jnp.float32)
 
-    r = iota((64, BLK), 0)
-    pos = iota((64, BLK), 1)
-    sel = (((r & 7) < CAP) & (pos == (r >> 3) * 6 + (r & 7))).astype(jnp.float32)
-    ret[:, :, :FEAT] = jnp.dot(
-        sel, rows, precision=HIGH, preferred_element_type=jnp.float32
-    ).reshape(EXPERTS, 8, FEAT)
+    for j in range(EXPERTS):
+        ret[j, :CAP, :FEAT] = rows[j * CAP : (j + 1) * CAP]
     ret[:, :, FEAT:] = jnp.broadcast_to(scs[...][None], (EXPERTS, 8, 128))
     for i in range(1, 8):
         e = lax.rem(own + i, 8)

time: 80.3 us -> 83.8 us (1.044)
  Pallas kernels: 76.9 us -> 80.4 us
    pallas_call x1, Pallas kernels: 76.9 us -> 80.4 us  [local(): pl.pallas_call(kernel, out_shape=(jax.ShapeDtypeStruct((TOK, FEAT), bf),...]
where the time goes in v5:
time: 83.8 us; the launch traced here: 83.6 us
  Pallas kernels  80.4 us (96%)
  local copies, waits for them, and re-layouts  2.52 us (3%)
    pallas_call x1, Pallas kernels, local(): pl.pallas_call(kernel, out_shape=(jax.ShapeDtypeStruct((TOK, FEAT), bf),...  80.4 us
    unnamed x2, local copies, waits for them, and re-layouts  2.52 us

profile of v5, /device:TPU:8, one launch (start us, length us, event | category | flops | bytes accessed | tf_op | source)
XLA Modules:
  0.0 83.6 jit_solution(5797846541150176728)
XLA Ops:
  0.6 80.4 %moe_dx.1 = (bf16[16,384]{1,0:T(8,128)(2,1)}, f32[2,16]{1,0:T(2,128)}) custom-call(bf16[16,384]{1,0:T(8,128)(2,1)} %tok_h.1, bf16[16,384]{1,0:T(8,128)(2,1)} %dout_h.1, f32[2,16]{1,0:T(2,128)} %bitcast.5, s32[2,16]{1,0:T(2,128)} %bitcast.6, s32[2,16]{1,0:T(2,128)} %bitcast.7, bf16[3072,256]{1,0:T(8,128)(2,1)} %wg.1, bf16[3072,256]{1,0:T(8,128)(2,1)} %wu.1, ...), custom_call_target="tpu_custom_call" | custom-call | flops 3019898880 | bytes 4718592 | tf_op jit(solution)/shard_map/moe_dx/pallas_call | solution.py:458
  81.1 1.3 %copy.12 = bf16[16,384]{1,0:T(8,128)(2,1)} copy(bf16[16,384]{1,0:T(8,128)(2,1)} %get-tuple-element.8) | data formatting | bytes 24576
  82.4 1.2 %copy.13 = f32[16,2]{0,1:T(2,128)} copy(f32[16,2]{0,1:T(2,128)} %bitcast.4) | data formatting | bytes 256

commit v6 on v4

--- a/solution.py
+++ b/solution.py
@@ -216,14 +216,15 @@
         )
 
     near = (1, 7, 2, 6, 3, 5, 4)
-    for i in near:
-        start(q_own(i))
     for i in range(1, 4):
         yy = lax.rem(yl + i, 4)
         start(over_y(i, yl, at_y(yy)))
+    for i in near[::-1]:
+        start(q_own(i))
     q_spread(0)
     acc_gu[...] = jnp.zeros_like(acc_gu)
     acc_b[...] = jnp.zeros_like(acc_b)
+    ret[...] = jnp.zeros_like(ret)
     for i in range(1, 4):
         yy = lax.rem(yl + 4 - i, 4)
         over_y(i, yy, at_y(yy)).wait_recv()
@@ -350,12 +351,8 @@
             copy(dst, dst, yy_ss.at[i, h], yy_rs.at[i, h], at_y(lax.rem(yl + 4 - i, 4))).wait_recv()
         rows = rows + yrecv[i].astype(jnp.float32)
 
-    r = iota((64, BLK), 0)
-    pos = iota((64, BLK), 1)
-    sel = (((r & 7) < CAP) & (pos == (r >> 3) * 6 + (r & 7))).astype(jnp.float32)
-    ret[:, :, :FEAT] = jnp.dot(
-        sel, rows, precision=HIGH, preferred_element_type=jnp.float32
-    ).reshape(EXPERTS, 8, FEAT)
+    for j in range(EXPERTS):
+        ret[j, :CAP, :FEAT] = rows[j * CAP : (j + 1) * CAP]
     ret[:, :, FEAT:] = jnp.broadcast_to(scs[...][None], (EXPERTS, 8, 128))
     for i in range(1, 8):
         e = lax.rem(own + i, 8)

time: 80.3 us -> 81.6 us (1.016)
  the two profiles are of different devices: /device:TPU:8 before, /device:TPU:73 now
where the time goes in v6:
time: 81.6 us; the launch traced here: 81.4 us
  Pallas kernels  78.2 us (96%)
  local copies, waits for them, and re-layouts  2.52 us (3%)
    pallas_call x1, Pallas kernels, local(): pl.pallas_call(kernel, out_shape=(jax.ShapeDtypeStruct((TOK, FEAT), bf),...  78.2 us
    unnamed x2, local copies, waits for them, and re-layouts  2.52 us

profile of v6, /device:TPU:73, one launch (start us, length us, event | category | flops | bytes accessed | tf_op | source)
XLA Modules:
  0.0 81.4 jit_solution(16273880659775516492)
XLA Ops:
  0.6 78.2 %moe_dx.1 = (bf16[16,384]{1,0:T(8,128)(2,1)}, f32[2,16]{1,0:T(2,128)}) custom-call(bf16[16,384]{1,0:T(8,128)(2,1)} %tok_h.1, bf16[16,384]{1,0:T(8,128)(2,1)} %dout_h.1, f32[2,16]{1,0:T(2,128)} %bitcast.5, s32[2,16]{1,0:T(2,128)} %bitcast.6, s32[2,16]{1,0:T(2,128)} %bitcast.7, bf16[3072,256]{1,0:T(8,128)(2,1)} %wg.1, bf16[3072,256]{1,0:T(8,128)(2,1)} %wu.1, ...), custom_call_target="tpu_custom_call" | custom-call | flops 3019898880 | bytes 4718592 | tf_op jit(solution)/shard_map/moe_dx/pallas_call | solution.py:446
  78.9 1.3 %copy.12 = bf16[16,384]{1,0:T(8,128)(2,1)} copy(bf16[16,384]{1,0:T(8,128)(2,1)} %get-tuple-element.8) | data formatting | bytes 24576
  80.2 1.2 %copy.13 = f32[16,2]{0,1:T(2,128)} copy(f32[16,2]{0,1:T(2,128)} %bitcast.4) | data formatting | bytes 256
